TPU v7x, 256 devices: a whole 4x4x8 slice. The times are simulated.
256 devices in a mesh: grid: 2 (over y_lo), lat: 16 (over y_hi, x, core), lon: 8 (over z).
Axes of the slice: x: 4, y: 4 (y_hi: 2, y_lo: 2; y = y_hi * 2 + y_lo), z: 8, core: 2. Of those that a mesh axis runs over, the one named last changes fastest.
Arguments:
- fields: bfloat16 [2, 768, 128, 1024], P('grid', None, 'lat', 'lon'), may hold values from -6 to 6
- cotangent: bfloat16 [2, 768, 128, 1024], P('grid', None, 'lat', 'lon'), may hold values from -6 to 6
- wet_mask: int32 [128, 1024], P('lat', 'lon'), may hold values 0 or 1
- atmos_kernel: float32 [384, 49], replicated, may hold values from -0.875 to 0.875
- atmos_gain: float32 [384], replicated, may hold values from 0.5 to 1.5
- atmos_shift: float32 [384], replicated, may hold values from -3 to 3
- atmos_w_in: bfloat16 [384, 1536], replicated, may hold values from -0.3125 to 0.3125
- atmos_b_in: float32 [1536], replicated, may hold values from -3 to 3
- atmos_w_out: bfloat16 [1536, 384], replicated, may hold values from -0.15625 to 0.15625
- atmos_b_out: float32 [384], replicated, may hold values from -3 to 3
- atmos_scale: float32 [384], replicated, may hold values from 0.5 to 1.5
- ocean_kernel: float32 [256, 49], replicated, may hold values from -0.875 to 0.875
- ocean_gain: float32 [256], replicated, may hold values from 0.5 to 1.5
- ocean_shift: float32 [256], replicated, may hold values from -3 to 3
- ocean_w_in: bfloat16 [256, 1024], replicated, may hold values from -0.375 to 0.375
- ocean_b_in: float32 [1024], replicated, may hold values from -3 to 3
- ocean_w_out: bfloat16 [1024, 256], replicated, may hold values from -0.1875 to 0.1875
- ocean_b_out: float32 [256], replicated, may hold values from -3 to 3
- ocean_scale: float32 [256], replicated, may hold values from 0.5 to 1.5
- sources: int32 [2, 16, 8, 3], P('grid', 'lat', 'lon'), may hold values from 0 to 7, as said below
- regrid: bfloat16 [2, 16, 8, 3, 8, 128, 128], P('grid', 'lat', 'lon'), may hold values from -0.3125 to 0.3125
Outputs:
- advanced: bfloat16 [2, 768, 128, 1024], P('grid', None, 'lat', 'lon')
- field_grads: bfloat16 [2, 768, 128, 1024], P('grid', None, 'lat', 'lon')
Inputs may be any that keep to these rules, and one draw needn't show every extreme that they name: `sources`: each tile lists 3 different tile columns of the other model in its own tile row.
All inputs are finite; a program needn't handle non-finite values. No bound on the sum of `wet_mask` on one device may be relied on, other than what follows from the above.
Results may differ from a plain program's by a relative error of at most 0.0049.
Values may be sent and summed in bfloat16 or wider, within the bound.
No kernel may reach another device: no remote copies, remote signals or barrier semaphores. Data moves between devices by JAX's collectives and lax.ppermute only.
A program may use at most 192 MiB of HBM per device.

v0:
```python
import functools
import math

import jax
import jax.numpy as jnp
from jax import lax
from jax.experimental import pallas as pl
from jax.experimental.pallas import tpu as pltpu
from jax.sharding import PartitionSpec as P

KF = 16
EPS = 1e-06
INV_ROOT_TWO = 1.0 / math.sqrt(2.0)
NORMAL_PEAK = 1.0 / math.sqrt(2.0 * math.pi)
HALF_LOG2E = 0.5 * math.log2(math.e)
BF = jnp.bfloat16
F32 = jnp.float32
VMEM = pl.BlockSpec(memory_space=pltpu.VMEM)
SMEM = pl.BlockSpec(memory_space=pltpu.SMEM)
ANY = pl.BlockSpec(memory_space=pl.ANY)
STEPS = 8
ROWS = 8
LON = 128
TALL = 14


def params(**extra):
    return pltpu.CompilerParams(vmem_limit_bytes=56 * 2**20, **extra)


def cost(flops, nbytes):
    return pl.CostEstimate(flops=flops, bytes_accessed=nbytes, transcendentals=0)


def swap(block, axes, move):
    sizes = [lax.axis_size(axis) for axis in axes]
    route = []
    total = math.prod(sizes)
    for start in range(total):
        place = []
        rest = start
        for size in reversed(sizes):
            place.insert(0, rest % size)
            rest //= size
        goal = 0
        for size, value in zip(sizes, move(*place)):
            goal = goal * size + value
        route.append((start, goal))
    return lax.ppermute(block, axes, route)


def even_swap(block, axis):
    return swap(block, (axis,), lambda i: (i ^ 1,))


def odd_swap(block, axis):
    count = lax.axis_size(axis)
    return swap(block, (axis,), lambda i: ((((i + 1) ^ 1) - 1) % count,))


def model_keep(wet_ref):
    wet = wet_ref[...].astype(F32)
    return jnp.where(lax.axis_index("grid") == 1, wet, jnp.ones_like(wet))


def prepare_kernel(field_ref, wet_ref, rows_ref, even_ref, odd_ref, surface_ref, scratch):
    chans = field_ref.shape[0]
    keep = model_keep(wet_ref)
    held = field_ref[...].astype(F32) * keep[None]
    scratch[...] = held.reshape(chans * ROWS, LON)
    for row in range(ROWS):
        rows_ref[row] = scratch[pl.ds(row, chans, stride=ROWS), :].astype(BF)
    parity = lax.rem(lax.axis_index("lat"), 2)

    @pl.when(parity == 0)
    def _():
        even_ref[...] = rows_ref[ROWS - 3 :]
        odd_ref[...] = rows_ref[:3]

    @pl.when(parity == 1)
    def _():
        even_ref[...] = rows_ref[:3]
        odd_ref[...] = rows_ref[ROWS - 3 :]

    @pl.when(pl.program_id(0) == 0)
    def _():
        surface_ref[...] = rows_ref[:, :KF, :]


def prepare(field, wet_mask):
    stacked = field.shape[0]
    part = 256
    return pl.pallas_call(
        prepare_kernel,
        grid=(stacked // part,),
        in_specs=[
            pl.BlockSpec((part, ROWS, LON), lambda s: (s, 0, 0)),
            pl.BlockSpec((ROWS, LON), lambda s: (0, 0)),
        ],
        out_specs=[
            pl.BlockSpec((ROWS, part, LON), lambda s: (0, s, 0)),
            pl.BlockSpec((3, part, LON), lambda s: (0, s, 0)),
            pl.BlockSpec((3, part, LON), lambda s: (0, s, 0)),
            pl.BlockSpec((ROWS, KF, LON), lambda s: (0, 0, 0)),
        ],
        out_shape=[
            jax.ShapeDtypeStruct((ROWS, stacked, LON), BF),
            jax.ShapeDtypeStruct((3, stacked, LON), BF),
            jax.ShapeDtypeStruct((3, stacked, LON), BF),
            jax.ShapeDtypeStruct((ROWS, KF, LON), BF),
        ],
        scratch_shapes=[pltpu.VMEM((part * ROWS, LON), F32)],
        compiler_params=params(),
        cost_estimate=cost(10**6, 5 * 10**6),
        name="prepare",
    )(field, wet_mask)


def scaled_kernel(cot_ref, wet_ref, scale_ref, out_ref, scratch):
    chans = cot_ref.shape[0]
    keep = model_keep(wet_ref)
    held = cot_ref[...].astype(F32) * keep[None]
    scratch[...] = held.reshape(chans * ROWS, LON)
    scale = jnp.broadcast_to(scale_ref[...], (chans, LON))
    for row in range(ROWS):
        out_ref[row] = (scale * scratch[pl.ds(row, chans, stride=ROWS), :]).astype(BF)


def scaled_cotangent(cot, wet_mask, scale_rows):
    stacked = cot.shape[0]
    part = 256
    return pl.pallas_call(
        scaled_kernel,
        grid=(stacked // part,),
        in_specs=[
            pl.BlockSpec((part, ROWS, LON), lambda s: (s, 0, 0)),
            pl.BlockSpec((ROWS, LON), lambda s: (0, 0)),
            pl.BlockSpec((part, 1), lambda s: (s, 0)),
        ],
        out_specs=pl.BlockSpec((ROWS, part, LON), lambda s: (0, s, 0)),
        out_shape=jax.ShapeDtypeStruct((ROWS, stacked, LON), BF),
        scratch_shapes=[pltpu.VMEM((part * ROWS, LON), F32)],
        compiler_params=params(),
        cost_estimate=cost(10**6, 4 * 10**6),
        name="scaled_cotangent",
    )(cot, wet_mask, scale_rows)


def bands_kernel(taps_ref, out_ref):
    lane = lax.broadcasted_iota(jnp.int32, (8, LON), 1)
    chan = lax.broadcasted_iota(jnp.int32, (8, LON), 0)
    for block in range(3):
        for col in range(7):
            firsts = []
            for half in range(2):
                start = block * 16 + half * 8
                taps = taps_ref[0, col, start : start + 8, :]
                firsts.append(jnp.where(lax.rem(lane, 16) == chan + 8 * half, taps, 0.0))
            for row in range(ROWS):
                low = []
                high = []
                for first in firsts:
                    moved = pltpu.roll(first, 16 * row, 1) if row else first
                    low.append(jnp.where(lane >= 16 * row, moved, 0.0))
                    high.append(jnp.where(lane < 16 * row, moved, 0.0))
                place = slice(row * 16, row * 16 + 16)
                out_ref[0, 0, block, col, place, :LON] = jnp.concatenate(low, 0).astype(BF)
                out_ref[0, 0, block, col, place, LON:] = jnp.concatenate(high, 0).astype(BF)


def bands(taps):
    return pl.pallas_call(
        bands_kernel,
        grid=(2, STEPS),
        in_specs=[pl.BlockSpec((1, 7, 48, LON), lambda d, s: (d, 0, s, 0))],
        out_specs=pl.BlockSpec((1, 1, 3, 7, LON, 2 * LON), lambda d, s: (d, s, 0, 0, 0, 0)),
        out_shape=jax.ShapeDtypeStruct((2, STEPS, 3, 7, LON, 2 * LON), BF),
        compiler_params=params(),
        cost_estimate=cost(10**6, 25 * 10**6),
        name="bands",
    )(taps)


def gather_rows_kernel(own_ref, even_ref, odd_ref, tall_ref, packed_ref):
    lat = lax.axis_index("lat")
    first = lax.rem(lat, 2) == 0
    top_live = (lat > 0).astype(F32)
    bottom_live = (lat < lax.axis_size("lat") - 1).astype(F32)
    for row in range(3):
        even = even_ref[row].astype(F32)
        odd = odd_ref[row].astype(F32)
        tall_ref[row] = (jnp.where(first, odd, even) * top_live).astype(BF)
        tall_ref[ROWS + 3 + row] = (jnp.where(first, even, odd) * bottom_live).astype(BF)
    tall_ref[3 : ROWS + 3] = own_ref[...]
    lane = lax.broadcasted_iota(jnp.int32, (16, LON), 1)
    outer = (lane < 3) | (lane >= LON - 3)
    for row in range(TALL):
        total = jnp.zeros((16, LON), F32)
        for block in range(16):
            values = tall_ref[row, block * 16 : block * 16 + 16, :].astype(F32)
            values = jnp.where(outer, values, 0.0)
            total = total + (pltpu.roll(values, 8 * block, 1) if block else values)
        packed_ref[row] = total.astype(BF)


def gather_rows(own, even, odd):
    stacked = own.shape[1]
    return pl.pallas_call(
        gather_rows_kernel,
        grid=(stacked // 256,),
        in_specs=[
            pl.BlockSpec((ROWS, 256, LON), lambda s: (0, s, 0)),
            pl.BlockSpec((3, 256, LON), lambda s: (0, s, 0)),
            pl.BlockSpec((3, 256, LON), lambda s: (0, s, 0)),
        ],
        out_specs=[
            pl.BlockSpec((TALL, 256, LON), lambda s: (0, s, 0)),
            pl.BlockSpec((TALL, 16, LON), lambda s: (0, s, 0)),
        ],
        out_shape=[
            jax.ShapeDtypeStruct((TALL, stacked, LON), BF),
            jax.ShapeDtypeStruct((TALL, stacked // 16, LON), BF),
        ],
        compiler_params=params(),
        cost_estimate=cost(10**6, 5 * 10**6),
        name="gather_rows",
    )(own, even, odd)


def convolve(tall_ref, outer_ref, band_ref, block, starts):
    lane = lax.broadcasted_iota(jnp.int32, (16, LON), 1)
    inner = []
    beyond = []
    for start in starts:
        place = pl.multiple_of(start, 16)
        index = start // 16
        lot = pl.multiple_of((index // 16) * 16, 16)
        turn = lax.rem(LON - 8 * lax.rem(index, 16), LON)
        inner.append([tall_ref[row, pl.ds(place, 16), :] for row in range(TALL)])
        beyond.append(
            [
                pltpu.roll(outer_ref[row, pl.ds(lot, 16), :], turn, 1).astype(BF)
                for row in range(TALL)
            ]
        )
    blank = jnp.zeros((32, LON), BF)
    total = None
    for col in range(7):
        shift = col - 3
        sides = []
        for mine, other in zip(inner, beyond):
            if shift > 0:
                mine = [jnp.where(lane < shift, o, m) for m, o in zip(mine, other)]
            elif shift < 0:
                mine = [jnp.where(lane >= LON + shift, o, m) for m, o in zip(mine, other)]
            sides.append(jnp.concatenate(mine + [blank], axis=0))
        spread = jnp.concatenate(sides, axis=1)
        terms = jnp.dot(band_ref[0, 0, block, col], spread, preferred_element_type=F32)
        moved = []
        for level in range(len(starts)):
            piece = terms[:, level * LON : (level + 1) * LON]
            moved.append(pltpu.roll(piece, (-shift) % LON, 1) if shift else piece)
        total = moved if total is None else [t + m for t, m in zip(total, moved)]
    return total


def merge_outer(even_ref, odd_ref, outer_ref):
    first = lax.rem(lax.axis_index("lon"), 2) == 0
    lane = lax.broadcasted_iota(jnp.int32, even_ref.shape[1:], 1)
    from_right = lax.rem(lane, 8) < 4
    for row in range(TALL):
        even = even_ref[row].astype(F32)
        odd = odd_ref[row].astype(F32)
        right = jnp.where(first, even, odd)
        left = jnp.where(first, odd, even)
        outer_ref[row] = jnp.where(from_right, right, left)


def over_blocks(chans, levels, body):
    step = pl.program_id(0)
    count = chans // 16 // STEPS
    for block in range(count):
        base = (step * count + block) * 16
        body(block, [base + level * chans for level in range(levels)])


def mixing_kernel(models, tall_ref, even_ref, odd_ref, band_ref, out_ref, outer_ref):
    @pl.when(pl.program_id(0) == 0)
    def _():
        merge_outer(even_ref, odd_ref, outer_ref)

    def body(block, starts):
        totals = convolve(tall_ref, outer_ref, band_ref, block, starts)
        for start, total in zip(starts, totals):
            place = pl.ds(pl.multiple_of(start, 16), 16)
            for row in range(ROWS):
                out_ref[row, place, :] = total[row * 16 : row * 16 + 16]

    for which, (chans, levels) in enumerate(models):

        @pl.when(lax.axis_index("grid") == which)
        def _():
            over_blocks(chans, levels, body)


def mixing(models, tall, even, odd, band):
    stacked = tall.shape[1]

    return pl.pallas_call(
        functools.partial(mixing_kernel, models),
        grid=(STEPS,),
        in_specs=[
            VMEM,
            VMEM,
            VMEM,
            pl.BlockSpec((1, 1, 3, 7, LON, 2 * LON), lambda s: (0, s, 0, 0, 0, 0)),
        ],
        out_specs=pl.BlockSpec((ROWS, stacked, LON), lambda s: (0, 0, 0)),
        out_shape=jax.ShapeDtypeStruct((ROWS, stacked, LON), F32),
        scratch_shapes=[pltpu.VMEM((TALL, stacked // 16, LON), F32)],
        compiler_params=params(),
        cost_estimate=cost(3 * 10**9, 18 * 10**6),
        name="mixing",
    )(tall, even, odd, band)


def adjoint_kernel(
    models, tall_ref, even_ref, odd_ref, band_ref, cot_ref, wet_ref, coupling_ref, out_ref, outer_ref
):
    @pl.when(pl.program_id(0) == 0)
    def _():
        merge_outer(even_ref, odd_ref, outer_ref)

    keep = model_keep(wet_ref)

    def body(block, starts):
        totals = convolve(tall_ref, outer_ref, band_ref, block, starts)
        for level, (start, total) in enumerate(zip(starts, totals)):
            place = pl.ds(pl.multiple_of(start, 16), 16)
            shaped = total.reshape(ROWS, 16, LON)
            if level == 0:
                live = (start == 0).astype(F32)
                shaped = shaped + coupling_ref[...].astype(F32) * live
            by_chan = jnp.swapaxes(shaped, 0, 1)
            cot = cot_ref[place].astype(F32)
            out_ref[place] = ((cot + by_chan) * keep[None]).astype(BF)

    for which, (chans, levels) in enumerate(models):

        @pl.when(lax.axis_index("grid") == which)
        def _():
            over_blocks(chans, levels, body)


def adjoint(models, tall, even, odd, band, cot, wet_mask, coupling):

    stacked = tall.shape[1]
    return pl.pallas_call(
        functools.partial(adjoint_kernel, models),
        grid=(STEPS,),
        in_specs=[
            VMEM,
            VMEM,
            VMEM,
            pl.BlockSpec((1, 1, 3, 7, LON, 2 * LON), lambda s: (1, s, 0, 0, 0, 0)),
            VMEM,
            VMEM,
            VMEM,
        ],
        out_specs=pl.BlockSpec((stacked, ROWS, LON), lambda s: (0, 0, 0)),
        out_shape=jax.ShapeDtypeStruct((stacked, ROWS, LON), BF),
        scratch_shapes=[pltpu.VMEM((TALL, stacked // 16, LON), F32)],
        compiler_params=params(),
        cost_estimate=cost(3 * 10**9, 18 * 10**6),
        name="adjoint",
    )(tall, even, odd, band, cot, wet_mask, coupling)


def slot_of(source):
    apart = source ^ lax.axis_index("lon")
    return ((apart & 1) << 2) | (apart & 2) | ((apart >> 2) & 1)


def cells_kernel(
    models,
    mixed_ref,
    rows_ref,
    up_ref,
    wet_ref,
    sources_ref,
    regrid_ref,
    pieces_ref,
    *rest,
):
    weights = rest[:12]
    advanced_ref, grad_ref, even_ref, odd_ref, terms_ref = rest[12:17]
    forcing_ref, kept_ref, unit_ref, act_ref, back_ref, *held = rest[17:]
    sems = held[-1]
    held = held[:-1]

    slots = [slot_of(sources_ref[0, p]) for p in range(3)]
    for row in range(ROWS):
        total = None
        for p in range(3):
            part = lax.dot_general(
                pieces_ref[slots[p], row],
                regrid_ref[p, row],
                (((1,), (1,)), ((), ())),
                preferred_element_type=F32,
            )
            total = part if total is None else total + part
        forcing_ref[row] = total
    terms_ref[...] = jnp.zeros_like(terms_ref)

    def run(which, chans, levels):
        in_t, out_n, out_t, in_n, bias_in, table = weights[6 * which : 6 * which + 6]
        hidden_units = out_n.shape[0]
        in_t_v, out_n_v, out_t_v, in_n_v, bias_v, gain_v, shift_v, bias_out_v, scale_v = held[
            9 * which : 9 * which + 9
        ]
        copies = [
            pltpu.make_async_copy(src, dst, sems.at[4 * which + k])
            for k, (src, dst) in enumerate(
                ((in_t, in_t_v), (out_n, out_n_v), (out_t, out_t_v), (in_n, in_n_v))
            )
        ]
        for copy in copies:
            copy.start()
        bias_v[...] = jnp.broadcast_to(bias_in[...], bias_v.shape)
        for k, ref in enumerate((gain_v, shift_v, bias_out_v, scale_v)):
            ref[...] = jnp.broadcast_to(table[:, k : k + 1], ref.shape)
        for copy in copies:
            copy.wait()
        share = 1.0 / chans
        wide = 2 * LON
        part = 256

        def pair(values):
            return jnp.concatenate([values, values], axis=1)

        def chunk(index, carry):
            level = index // 4
            row = lax.rem(index, 4) * 2
            base = pl.multiple_of(level * chans, 16)
            place = pl.ds(base, chans)
            live = (level == 0).astype(F32)
            normed = []
            inverses = []
            for k in range(2):
                mixed = mixed_ref[row + k, place, :]
                top = mixed[:KF] + forcing_ref[row + k] * live
                mixed = jnp.concatenate([top, mixed[KF:]], axis=0)
                centre = jnp.sum(mixed, axis=0, keepdims=True) * share
                spread = mixed - centre
                inverse = lax.rsqrt(jnp.sum(spread * spread, axis=0, keepdims=True) * share + EPS)
                unit = spread * inverse
                unit_ref[k, :chans, :] = unit
                inverses.append(inverse)
                normed.append((unit * gain_v[...] + shift_v[...]).astype(BF))
            normed = jnp.concatenate(normed, axis=1)
            up = jnp.concatenate([up_ref[row, place, :], up_ref[row + 1, place, :]], axis=1)
            for start in range(0, hidden_units, part):
                these = slice(start, start + part)
                hidden = jnp.dot(in_t_v[these, :], normed, preferred_element_type=F32)
                active_grad = jnp.dot(out_n_v[these, :], up, preferred_element_type=F32)
                hidden = hidden + pair(bias_v[these, :])
                below = 0.5 + 0.5 * lax.erf(hidden * INV_ROOT_TWO)
                act_ref[these, :] = (hidden * below).astype(BF)
                bell = jnp.exp2((hidden * hidden) * -HALF_LOG2E) * NORMAL_PEAK
                back_ref[these, :] = (active_grad * (below + hidden * bell)).astype(BF)
            update = jnp.dot(
                out_t_v[...], act_ref[:hidden_units, :], preferred_element_type=F32
            )
            normed_grad = jnp.dot(
                in_n_v[...], back_ref[:hidden_units, :], preferred_element_type=F32
            )
            for k in range(2):
                lanes = slice(k * LON, (k + 1) * LON)
                moved = scale_v[...] * (update[:, lanes] + bias_out_v[...])
                kept_ref[row + k, place, :] = rows_ref[row + k, place, :].astype(F32) + moved
                scaled = normed_grad[:, lanes] * gain_v[...]
                unit = unit_ref[k, :chans, :]
                mean = jnp.sum(scaled, axis=0, keepdims=True) * share
                slope = jnp.sum(scaled * unit, axis=0, keepdims=True) * share
                grad = (inverses[k] * (scaled - mean - unit * slope)).astype(BF)
                grad_ref[row + k, place, :] = grad

                @pl.when(level == 0)
                def _():
                    for p in range(3):
                        terms_ref[slots[p], row + k] = jnp.dot(
                            grad[:KF], regrid_ref[p, row + k], preferred_element_type=F32
                        ).astype(BF)

            return carry

        lax.fori_loop(0, levels * 4, chunk, 0)

    for which, (chans, levels) in enumerate(models):

        @pl.when(lax.axis_index("grid") == which)
        def _():
            run(which, chans, levels)

    keep = model_keep(wet_ref)

    def finish(index, carry):
        place = pl.ds(pl.multiple_of(index * 16, 16), 16)
        by_chan = jnp.swapaxes(kept_ref[:, place, :], 0, 1)
        advanced_ref[place] = (by_chan * keep[None]).astype(BF)
        return carry

    lax.fori_loop(0, kept_ref.shape[1] // 16, finish, 0)
    parity = lax.rem(lax.axis_index("lat"), 2)

    @pl.when(parity == 0)
    def _():
        even_ref[...] = grad_ref[ROWS - 3 :]
        odd_ref[...] = grad_ref[:3]

    @pl.when(parity == 1)
    def _():
        even_ref[...] = grad_ref[:3]
        odd_ref[...] = grad_ref[ROWS - 3 :]


def cells(models, mixed, rows, up, wet_mask, sources, regrid, pieces, weights):

    stacked = rows.shape[1]
    held = []
    for which in range(2):
        in_t, out_n, out_t, in_n, bias_in, table = weights[6 * which : 6 * which + 6]
        held += [pltpu.VMEM(w.shape, BF) for w in (in_t, out_n, out_t, in_n)]
        held.append(pltpu.VMEM((bias_in.shape[0], LON), F32))
        held += [pltpu.VMEM((table.shape[0], LON), F32)] * 4
    most_chans = max(chans for chans, _ in models)
    most_units = max(weights[1].shape[0], weights[7].shape[0])
    return pl.pallas_call(
        functools.partial(cells_kernel, models),
        in_specs=[VMEM, VMEM, VMEM, VMEM, SMEM, VMEM, VMEM] + ([ANY] * 4 + [VMEM] * 2) * 2,
        out_specs=[VMEM] * 5,
        out_shape=[
            jax.ShapeDtypeStruct((stacked, ROWS, LON), BF),
            jax.ShapeDtypeStruct((ROWS, stacked, LON), BF),
            jax.ShapeDtypeStruct((3, stacked, LON), BF),
            jax.ShapeDtypeStruct((3, stacked, LON), BF),
            jax.ShapeDtypeStruct((8, ROWS, KF, LON), BF),
        ],
        scratch_shapes=[
            pltpu.VMEM((ROWS, KF, LON), F32),
            pltpu.VMEM((ROWS, stacked, LON), F32),
            pltpu.VMEM((2, most_chans, LON), F32),
            pltpu.VMEM((most_units, 2 * LON), BF),
            pltpu.VMEM((most_units, 2 * LON), BF),
        ]
        + held
        + [pltpu.SemaphoreType.DMA((8,))],
        compiler_params=params(),
        cost_estimate=cost(10**10, 20 * 10**6),
        name="cells",
    )(mixed, rows, up, wet_mask, sources, regrid, pieces, *weights)


def gather_surfaces(surface):
    block = swap(surface[None], ("grid",), lambda g: (1 - g,))
    for apart in (4, 2, 1):
        block = jnp.concatenate(
            [block, swap(block, ("lon",), lambda j, apart=apart: (j ^ apart,))], axis=0
        )
    return block


def scatter_terms(terms):
    for apart in (1, 2, 4):
        half = terms.shape[0] // 2
        came = swap(terms[half:], ("lon",), lambda j, apart=apart: (j ^ apart,))
        terms = (terms[:half].astype(F32) + came.astype(F32)).astype(BF)
    return swap(terms, ("grid",), lambda g: (1 - g,))[0]


def per_device(
    fields,
    cotangent,
    wet_mask,
    atmos_kernel,
    atmos_gain,
    atmos_shift,
    atmos_w_in,
    atmos_b_in,
    atmos_w_out,
    atmos_b_out,
    atmos_scale,
    ocean_kernel,
    ocean_gain,
    ocean_shift,
    ocean_w_in,
    ocean_b_in,
    ocean_w_out,
    ocean_b_out,
    ocean_scale,
    sources,
    regrid,
):
    stacked = fields.shape[1]
    models = tuple((w.shape[0], stacked // w.shape[0]) for w in (atmos_w_in, ocean_w_in))
    is_ocean = lax.axis_index("grid") == 1
    field, cot = fields[0], cotangent[0]
    rows, even, odd, surface = prepare(field, wet_mask)
    even = even_swap(even, "lat")
    odd = odd_swap(odd, "lat")
    pieces = gather_surfaces(surface)

    most, taken = atmos_kernel.shape
    by_step = ocean_kernel.reshape(STEPS, ocean_kernel.shape[0] // STEPS, taken)
    spare = most // STEPS - by_step.shape[1]
    ocean_steps = jnp.pad(by_step, ((0, 0), (0, spare), (0, 0))).reshape(most, taken)
    kernel = jnp.where(is_ocean, ocean_steps, atmos_kernel)
    both = jnp.stack([kernel, kernel[:, ::-1]]).reshape(2, most, 7, 7)
    both = jnp.pad(both.transpose(0, 3, 1, 2), ((0, 0), (0, 0), (0, 0), (0, 1)))
    taps = jnp.repeat(both, 16, axis=3)
    band = bands(taps)
    scale_rows = jnp.where(
        is_ocean,
        jnp.tile(ocean_scale, models[1][1]),
        jnp.tile(atmos_scale, models[0][1]),
    )
    up = scaled_cotangent(cot, wet_mask, scale_rows[:, None])
    weights = []
    for w_in, w_out, b_in, columns in (
        (atmos_w_in, atmos_w_out, atmos_b_in, (atmos_gain, atmos_shift, atmos_b_out, atmos_scale)),
        (ocean_w_in, ocean_w_out, ocean_b_in, (ocean_gain, ocean_shift, ocean_b_out, ocean_scale)),
    ):
        weights += [w_in.T, w_out, w_out.T, w_in, b_in[:, None], jnp.stack(columns, axis=1)]

    tall, packed = gather_rows(rows, even, odd)
    mixed = mixing(models, tall, even_swap(packed, "lon"), odd_swap(packed, "lon"), band)
    advanced, grad, even, odd, terms = cells(
        models, mixed, rows, up, wet_mask, sources[0, 0], regrid[0, 0, 0], pieces, weights
    )
    even = even_swap(even, "lat")
    odd = odd_swap(odd, "lat")
    coupling = scatter_terms(terms)
    tall, packed = gather_rows(grad, even, odd)
    field_grads = adjoint(
        models,
        tall,
        even_swap(packed, "lon"),
        odd_swap(packed, "lon"),
        band,
        cot,
        wet_mask,
        coupling,
    )
    return (advanced[None], field_grads[None])


def solution(mesh):
    placed = (
        (P("grid", None, "lat", "lon"),) * 2
        + (P("lat", "lon"),)
        + (P(),) * 16
        + (P("grid", "lat", "lon", None), P("grid", "lat", "lon", None, None, None, None))
    )
    return jax.shard_map(
        per_device,
        mesh=mesh,
        in_specs=placed,
        out_specs=(P("grid", None, "lat", "lon"), P("grid", None, "lat", "lon")),
        check_vma=False,
    )
```

profile of v0, /device:TPU:32, one launch (start us, length us, event | category | flops | bytes accessed | tf_op | source)
XLA Modules:
  0.0 152.1 jit_solution(6350193153351512490)
XLA Ops:
  0.7 4.1 %prepare.1 = (bf16[8,768,128]{2,1,0:T(8,128)(2,1)}, bf16[3,768,128]{2,1,0:T(8,128)(2,1)}, bf16[3,768,128]{2,1,0:T(8,128)(2,1)}, bf16[8,16,128]{2,1,0:T(8,128)(2,1)}) custom-call(bf16[768,8,128]{2,1,0:T(8,128)(2,1)} %bitcast.41, s32[8,128]{1,0:T(8,128)} %wet_ref.7), custom_call_target="tpu_custom_call" | custom-call | flops 1000000 | bytes 5000000 | tf_op jit(solution)/shard_map/prepare/pallas_call | solution.py:93
  4.7 1.7 %collective-permute-start.4 = (bf16[1,8,16,128]{3,2,1,0:T(8,128)(2,1)}, bf16[1,8,16,128]{3,2,1,0:T(8,128)(2,1)S(1)}, u32[]{:S(2)}, u32[]{:S(2)}) collective-permute-start(bf16[1,8,16,128]{3,2,1,0:T(8,128)(2,1)} %bitcast.58), channel_id=1, source_target_pairs={{0,128},{128,0},{1,129},{129,1},{2,130},{130,2},{3,131},{131,3},{4... | collective-permute-start | bytes 98312 | tf_op jit(solution)/shard_map/ppermute | solution.py:49
  6.4 5.2 %collective-permute-start.1 = (bf16[3,768,128]{2,1,0:T(8,128)(2,1)}, bf16[3,768,128]{2,1,0:T(8,128)(2,1)S(1)}, u32[]{:S(2)}, u32[]{:S(2)}) collective-permute-start(bf16[3,768,128]{2,1,0:T(8,128)(2,1)} %get-tuple-element.17), channel_id=1, source_target_pairs={{0,120},{8,16},{16,8},{24,32},{32,24},{40,48},{48,40},{56,64},{64,... | collective-permute-start | bytes 1769480 | tf_op jit(solution)/shard_map/ppermute | solution.py:49
  11.6 0.2 copy.65
  11.8 0.0 copy-start.19
  11.8 0.0 copy-start.20
  11.9 0.0 copy-start.21
  11.9 0.2 copy.67
  12.1 0.8 bitcast_select_fusion.scale_ref
  12.9 0.1 copy.48
  13.0 0.1 copy.62
  13.1 6.4 %collective-permute-start.5 = (bf16[1,8,16,128]{3,2,1,0:T(8,128)(2,1)S(1)}, bf16[1,8,16,128]{3,2,1,0:T(8,128)(2,1)S(1)}, u32[]{:S(2)}, u32[]{:S(2)}) collective-permute-start(bf16[1,8,16,128]{3,2,1,0:T(8,128)(2,1)S(1)} %collective-permute-done.4), channel_id=1, source_target_pairs={{0,4},{1,5},{2,6},{3,7},{4,0},{5,1},{6,2},{7,3},{8,12},{9,13},{10,... | collective-permute-start | bytes 98312 | tf_op jit(solution)/shard_map/ppermute | solution.py:49
  19.5 0.1 rev.3
  19.8 1.8 %collective-permute-done.5 = bf16[1,8,16,128]{3,2,1,0:T(8,128)(2,1)S(1)} collective-permute-done((bf16[1,8,16,128]{3,2,1,0:T(8,128)(2,1)S(1)}, bf16[1,8,16,128]{3,2,1,0:T(8,128)(2,1)S(1)}, u32[]{:S(2)}, u32[]{:S(2)}) %collective-permute-start.5) | collective-permute-done | bytes 32800 | tf_op jit(solution)/shard_map/ppermute | solution.py:49
  21.6 2.8 %collective-permute-start.6 = (bf16[2,8,16,128]{3,2,1,0:T(8,128)(2,1)S(1)}, bf16[2,8,16,128]{3,2,1,0:T(8,128)(2,1)S(1)}, u32[]{:S(2)}, u32[]{:S(2)}) collective-permute-start(bf16[2,8,16,128]{3,2,1,0:T(8,128)(2,1)S(1)} %pad_maximum_fusion.2), channel_id=1, source_target_pairs={{0,2},{1,3},{2,0},{3,1},{4,6},{5,7},{6,4},{7,5},{8,10},{9,11},{10,... | collective-permute-start | bytes 196616 | tf_op jit(solution)/shard_map/ppermute | solution.py:49
  24.4 0.0 copy-start.22
  24.5 0.0 copy-start.23
  24.5 0.0 copy-start.24
  24.5 2.7 %collective-permute-done.6 = bf16[2,8,16,128]{3,2,1,0:T(8,128)(2,1)S(1)} collective-permute-done((bf16[2,8,16,128]{3,2,1,0:T(8,128)(2,1)S(1)}, bf16[2,8,16,128]{3,2,1,0:T(8,128)(2,1)S(1)}, u32[]{:S(2)}, u32[]{:S(2)}) %collective-permute-start.6) | collective-permute-done | bytes 65568 | tf_op jit(solution)/shard_map/ppermute | solution.py:49
  27.2 0.7 pad_maximum_fusion.1
  27.8 1.5 collective-permute-start.7
  29.3 0.0 copy-start.2
  29.4 0.8 copy-done.2
  30.2 0.2 copy-done.3
  30.4 4.8 %gather_rows.2 = (bf16[14,768,128]{2,1,0:T(8,128)(2,1)}, bf16[14,48,128]{2,1,0:T(8,128)(2,1)}) custom-call(bf16[8,768,128]{2,1,0:T(8,128)(2,1)} %get-tuple-element.15.own_ref.rows_ref, bf16[3,768,128]{2,1,0:T(8,128)(2,1)} %copy-done.2, bf16[3,768,128]{2,1,0:T(8,128)(2,1)} %copy-done.3), custom_call_target="tpu_custom_call" | custom-call | flops 1000000 | bytes 5000000 | tf_op jit(solution)/shard_map/gather_rows/pallas_call | solution.py:208
  35.2 2.1 %collective-permute-start.3 = (bf16[14,48,128]{2,1,0:T(8,128)(2,1)}, bf16[14,48,128]{2,1,0:T(8,128)(2,1)}, u32[]{:S(2)}, u32[]{:S(2)}) collective-permute-start(bf16[14,48,128]{2,1,0:T(8,128)(2,1)} %get-tuple-element.19), channel_id=1, source_target_pairs={{0,7},{1,2},{2,1},{3,4},{4,3},{5,6},{6,5},{7,0},{8,15},{9,10},{10,... | collective-permute-start | bytes 516104 | tf_op jit(solution)/shard_map/ppermute | solution.py:49
  37.3 3.4 %collective-permute-start.2 = (bf16[14,48,128]{2,1,0:T(8,128)(2,1)}, bf16[14,48,128]{2,1,0:T(8,128)(2,1)}, u32[]{:S(2)}, u32[]{:S(2)}) collective-permute-start(bf16[14,48,128]{2,1,0:T(8,128)(2,1)} %get-tuple-element.19), channel_id=1, source_target_pairs={{0,1},{1,0},{2,3},{3,2},{4,5},{5,4},{6,7},{7,6},{8,9},{9,8},{10,11... | collective-permute-start | bytes 516104 | tf_op jit(solution)/shard_map/ppermute | solution.py:49
  40.7 0.8 copy.61.rest_11_
  41.5 0.0 copy-start.15
  41.6 0.8 copy.59.rest_5_
  42.4 1.1 copy.60.rest_10_
  43.5 1.0 copy.56
  44.5 1.0 copy.57
  45.5 1.2 broadcast_in_dim.25.rest_4_
  46.7 1.4 copy.54
  48.1 1.5 copy.55
  49.6 0.2 broadcast_in_dim.19
  49.8 2.2 %copy.51.taps_ref = f32[2,7,384,128]{3,2,1,0:T(8,128)} copy(f32[2,7,384,128]{2,3,1,0:T(8,128)S(1)} %bitcast.38) | data formatting | bytes 5505024 | tf_op jit(solution)/shard_map/reshape | solution.py:620
  52.0 14.1 %bands.1.band_ref = bf16[2,8,3,7,128,256]{5,4,3,2,1,0:T(8,128)(2,1)} custom-call(f32[2,7,384,128]{3,2,1,0:T(8,128)} %copy.51.taps_ref), custom_call_target="tpu_custom_call" | custom-call | flops 1000000 | bytes 25000000 | tf_op jit(solution)/shard_map/bands/pallas_call | solution.py:172
  66.1 3.9 %scaled_cotangent.1.up_ref = bf16[8,768,128]{2,1,0:T(8,128)(2,1)} custom-call(bf16[768,8,128]{2,1,0:T(8,128)(2,1)} %bitcast.39, s32[8,128]{1,0:T(8,128)} %wet_ref.7, f32[768,1]{1,0:T(8,128)} %bitcast_select_fusion.scale_ref), custom_call_target="tpu_custom_call" | custom-call | flops 1000000 | bytes 4000000 | tf_op jit(solution)/shard_map/scaled_cotangent/pallas_call | solution.py:132
  70.0 1.6 %pad_maximum_fusion.pieces_ref = bf16[8,8,16,128]{3,2,1,0:T(8,128)(2,1)} fusion(bf16[4,8,16,128]{3,2,1,0:T(8,128)(2,1)} %collective-permute-done.7, bf16[2,8,16,128]{3,2,1,0:T(8,128)(2,1)S(1)} %copy-done.9, bf16[1,8,16,128]{3,2,1,0:T(8,128)(2,1)S(1)} %collective-permute-done.5, bf16[1,8,16,128]{3,2,1,0:T(8,128)(2,1)S(1)} %collective-permute-done.4), kind=kLoop, calls=%fused_computation.1 | loop fusion | flops 393216 | bytes 524288 | tf_op jit(solution)/shard_map/concatenate | solution.py:567
  71.7 13.2 %mixing.1.mixed_ref = f32[8,768,128]{2,1,0:T(8,128)} custom-call(bf16[14,768,128]{2,1,0:T(8,128)(2,1)} %get-tuple-element.18.tall_ref, bf16[14,48,128]{2,1,0:T(8,128)(2,1)} %collective-permute-done.2.even_ref, bf16[14,48,128]{2,1,0:T(8,128)(2,1)} %collective-permute-done.3.odd_ref, bf16[2,8,3,7,128,256]{5,4,3,2,1,0:T(8,128)(2,1)} %bands.1.band_ref), custom_call_target="tpu_custom_call" | custom-call | flops 3000000000 | bytes 18000000 | tf_op jit(solution)/shard_map/mixing/pallas_call | solution.py:309
  84.9 26.3 %cells.1 = (bf16[768,8,128]{2,1,0:T(8,128)(2,1)}, bf16[8,768,128]{2,1,0:T(8,128)(2,1)}, bf16[3,768,128]{2,1,0:T(8,128)(2,1)}, bf16[3,768,128]{2,1,0:T(8,128)(2,1)}, bf16[8,8,16,128]{3,2,1,0:T(8,128)(2,1)}) custom-call(f32[8,768,128]{2,1,0:T(8,128)} %mixing.1.mixed_ref, bf16[8,768,128]{2,1,0:T(8,128)(2,1)} %get-tuple-element.15.own_ref.rows_ref, ...), custom_call_target="tpu_custom_call" | custom-call | flops 10000000000 | bytes 20000000 | tf_op jit(solution)/shard_map/cells/pallas_call | solution.py:538
  111.2 0.9 slice.19
  112.1 0.1 collective-permute-start.12
  112.2 0.1 collective-permute-start.8
  112.3 0.4 collective-permute-start.9
  112.8 4.7 %collective-permute-done.12 = bf16[4,8,16,128]{3,2,1,0:T(8,128)(2,1)S(1)} collective-permute-done((bf16[4,8,16,128]{3,2,1,0:T(8,128)(2,1)S(1)}, bf16[4,8,16,128]{3,2,1,0:T(8,128)(2,1)S(1)}, u32[]{:S(2)}, u32[]{:S(2)}) %collective-permute-start.12) | collective-permute-done | bytes 131104 | tf_op jit(solution)/shard_map/ppermute | solution.py:49
  117.4 0.9 add_convert_fusion
  118.4 0.3 collective-permute-start.13
  118.7 5.0 %collective-permute-done.13 = bf16[2,8,16,128]{3,2,1,0:T(8,128)(2,1)S(1)} collective-permute-done((bf16[2,8,16,128]{3,2,1,0:T(8,128)(2,1)S(1)}, bf16[2,8,16,128]{3,2,1,0:T(8,128)(2,1)S(1)}, u32[]{:S(2)}, u32[]{:S(2)}) %collective-permute-start.13) | collective-permute-done | bytes 65568 | tf_op jit(solution)/shard_map/ppermute | solution.py:49
  123.7 1.4 collective-permute-start.14
  125.1 0.5 collective-permute-done.9.odd_ref
  125.6 0.3 copy-done.4
  125.9 0.5 copy-done.5
  126.4 4.8 %gather_rows.3 = (bf16[14,768,128]{2,1,0:T(8,128)(2,1)}, bf16[14,48,128]{2,1,0:T(8,128)(2,1)}) custom-call(bf16[8,768,128]{2,1,0:T(8,128)(2,1)} %get-tuple-element.22.own_ref, bf16[3,768,128]{2,1,0:T(8,128)(2,1)} %copy-done.4, bf16[3,768,128]{2,1,0:T(8,128)(2,1)} %copy-done.5), custom_call_target="tpu_custom_call" | custom-call | flops 1000000 | bytes 5000000 | tf_op jit(solution)/shard_map/gather_rows/pallas_call | solution.py:208
  131.1 1.0 collective-permute-start.11
  132.1 1.8 %collective-permute-start.10 = (bf16[14,48,128]{2,1,0:T(8,128)(2,1)}, bf16[14,48,128]{2,1,0:T(8,128)(2,1)S(1)}, u32[]{:S(2)}, u32[]{:S(2)}) collective-permute-start(bf16[14,48,128]{2,1,0:T(8,128)(2,1)} %get-tuple-element.26), channel_id=1, source_target_pairs={{0,1},{1,0},{2,3},{3,2},{4,5},{5,4},{6,7},{7,6},{8,9},{9,8},{10,11... | collective-permute-start | bytes 516104 | tf_op jit(solution)/shard_map/ppermute | solution.py:49
  133.9 0.1 collective-permute-start.15
  134.0 3.9 %collective-permute-done.15 = bf16[1,8,16,128]{3,2,1,0:T(8,128)(2,1)S(1)} collective-permute-done((bf16[1,8,16,128]{3,2,1,0:T(8,128)(2,1)S(1)}, bf16[1,8,16,128]{3,2,1,0:T(8,128)(2,1)S(1)}, u32[]{:S(2)}, u32[]{:S(2)}) %collective-permute-start.15) | collective-permute-done | bytes 32800 | tf_op jit(solution)/shard_map/ppermute | solution.py:49
  138.0 0.6 copy-done.14
  138.6 0.1 copy-done.10
  138.6 0.1 copy-done.11
  138.7 13.4 %adjoint.1 = bf16[768,8,128]{2,1,0:T(8,128)(2,1)} custom-call(bf16[14,768,128]{2,1,0:T(8,128)(2,1)} %get-tuple-element.25.tall_ref, bf16[14,48,128]{2,1,0:T(8,128)(2,1)} %copy-done.11, bf16[14,48,128]{2,1,0:T(8,128)(2,1)} %copy-done.10, bf16[2,8,3,7,128,256]{5,4,3,2,1,0:T(8,128)(2,1)} %bands.1.band_ref, bf16[768,8,128]{2,1,0:T(8,128)(2,1)} %bitcast.40, ...), custom_call_target="tpu_custom_call" | custom-call | flops 3000000000 | bytes 18000000 | tf_op jit(solution)/shard_map/adjoint/pallas_call | solution.py:358
  (68 shorter events, 0.3 us)
Async XLA Ops:
  0.6 11.0 %copy-start.16 = (f32[384]{0:T(512)S(1)}, f32[384]{0:T(512)}, u32[]{:S(2)}) copy-start(f32[384]{0:T(512)} %param.31) | copy-start | bytes 4612
  0.6 11.0 %copy-start.18 = (f32[256]{0:T(256)S(1)}, f32[256]{0:T(256)}, u32[]{:S(2)}) copy-start(f32[256]{0:T(256)} %param.39) | copy-start | bytes 3076
  0.7 12.2 %copy-start.13 = (f32[256,49]{0,1:T(8,128)S(1)}, f32[256,49]{0,1:T(8,128)}, u32[]{:S(2)}) copy-start(f32[256,49]{0,1:T(8,128)} %param.32) | copy-start | bytes 150532
  4.7 14.8 %copy-start.12 = (f32[384,49]{0,1:T(8,128)S(1)}, f32[384,49]{0,1:T(8,128)}, u32[]{:S(2)}) copy-start(f32[384,49]{0,1:T(8,128)} %param.24) | copy-start | bytes 225796
  4.7 8.4 %collective-permute-start.4 = (bf16[1,8,16,128]{3,2,1,0:T(8,128)(2,1)}, bf16[1,8,16,128]{3,2,1,0:T(8,128)(2,1)S(1)}, u32[]{:S(2)}, u32[]{:S(2)}) collective-permute-start(bf16[1,8,16,128]{3,2,1,0:T(8,128)(2,1)} %bitcast.58), channel_id=1, source_target_pairs={{0,128},{128,0},{1,129},{129,1},{2,130},{130,2},{3,131},{131,3},{4... | collective-permute-start | bytes 98312 | tf_op jit(solution)/shard_map/ppermute | solution.py:49
  6.4 22.9 %collective-permute-start = (bf16[3,768,128]{2,1,0:T(8,128)(2,1)}, bf16[3,768,128]{2,1,0:T(8,128)(2,1)S(1)}, u32[]{:S(2)}, u32[]{:S(2)}) collective-permute-start(bf16[3,768,128]{2,1,0:T(8,128)(2,1)} %get-tuple-element.16), channel_id=1, source_target_pairs={{0,8},{8,0},{16,24},{24,16},{32,40},{40,32},{48,56},{56,48},{64,72... | collective-permute-start | bytes 1769480 | tf_op jit(solution)/shard_map/ppermute | solution.py:49
  6.4 23.0 %collective-permute-start.1 = (bf16[3,768,128]{2,1,0:T(8,128)(2,1)}, bf16[3,768,128]{2,1,0:T(8,128)(2,1)S(1)}, u32[]{:S(2)}, u32[]{:S(2)}) collective-permute-start(bf16[3,768,128]{2,1,0:T(8,128)(2,1)} %get-tuple-element.17), channel_id=1, source_target_pairs={{0,120},{8,16},{16,8},{24,32},{32,24},{40,48},{48,40},{56,64},{64,... | collective-permute-start | bytes 1769480 | tf_op jit(solution)/shard_map/ppermute | solution.py:49
  11.8 7.9 %copy-start.19 = (f32[384]{0:T(512)S(1)}, f32[384]{0:T(512)}, u32[]{:S(2)}) copy-start(f32[384]{0:T(512)} %param.25) | copy-start | bytes 4612
  11.8 7.9 %copy-start.20 = (f32[384]{0:T(512)S(1)}, f32[384]{0:T(512)}, u32[]{:S(2)}) copy-start(f32[384]{0:T(512)} %param.26) | copy-start | bytes 4612
  11.9 7.9 %copy-start.21 = (f32[384]{0:T(512)S(1)}, f32[384]{0:T(512)}, u32[]{:S(2)}) copy-start(f32[384]{0:T(512)} %param.30) | copy-start | bytes 4612
  13.1 8.5 %collective-permute-start.5 = (bf16[1,8,16,128]{3,2,1,0:T(8,128)(2,1)S(1)}, bf16[1,8,16,128]{3,2,1,0:T(8,128)(2,1)S(1)}, u32[]{:S(2)}, u32[]{:S(2)}) collective-permute-start(bf16[1,8,16,128]{3,2,1,0:T(8,128)(2,1)S(1)} %collective-permute-done.4), channel_id=1, source_target_pairs={{0,4},{1,5},{2,6},{3,7},{4,0},{5,1},{6,2},{7,3},{8,12},{9,13},{10,... | collective-permute-start | bytes 98312 | tf_op jit(solution)/shard_map/ppermute | solution.py:49
  21.6 5.5 %collective-permute-start.6 = (bf16[2,8,16,128]{3,2,1,0:T(8,128)(2,1)S(1)}, bf16[2,8,16,128]{3,2,1,0:T(8,128)(2,1)S(1)}, u32[]{:S(2)}, u32[]{:S(2)}) collective-permute-start(bf16[2,8,16,128]{3,2,1,0:T(8,128)(2,1)S(1)} %pad_maximum_fusion.2), channel_id=1, source_target_pairs={{0,2},{1,3},{2,0},{3,1},{4,6},{5,7},{6,4},{7,5},{8,10},{9,11},{10,... | collective-permute-start | bytes 196616 | tf_op jit(solution)/shard_map/ppermute | solution.py:49
  24.4 16.2 %copy-start.22 = (f32[256]{0:T(256)S(1)}, f32[256]{0:T(256)}, u32[]{:S(2)}) copy-start(f32[256]{0:T(256)} %param.38) | copy-start | bytes 3076
  24.5 16.2 %copy-start.23 = (f32[256]{0:T(256)S(1)}, f32[256]{0:T(256)}, u32[]{:S(2)}) copy-start(f32[256]{0:T(256)} %param.34) | copy-start | bytes 3076
  24.5 16.2 %copy-start.24 = (f32[256]{0:T(256)S(1)}, f32[256]{0:T(256)}, u32[]{:S(2)}) copy-start(f32[256]{0:T(256)} %param.33) | copy-start | bytes 3076
  27.2 14.3 %copy-start.8 = (bf16[2,8,16,128]{3,2,1,0:T(8,128)(2,1)}, bf16[2,8,16,128]{3,2,1,0:T(8,128)(2,1)S(1)}, u32[]{:S(2)}) copy-start(bf16[2,8,16,128]{3,2,1,0:T(8,128)(2,1)S(1)} %collective-permute-done.6) | copy-start | bytes 196612
  27.8 42.2 %collective-permute-start.7 = (bf16[4,8,16,128]{3,2,1,0:T(8,128)(2,1)}, bf16[4,8,16,128]{3,2,1,0:T(8,128)(2,1)}, u32[]{:S(2)}, u32[]{:S(2)}) collective-permute-start(bf16[4,8,16,128]{3,2,1,0:T(8,128)(2,1)} %pad_maximum_fusion.1), channel_id=1, source_target_pairs={{0,1},{1,0},{2,3},{3,2},{4,5},{5,4},{6,7},{7,6},{8,9},{9,8},{10,11... | collective-permute-start | bytes 393224 | tf_op jit(solution)/shard_map/ppermute | solution.py:49
  29.3 0.8 copy-start.2
  29.4 1.0 copy-start.3
  30.4 12.1 %copy-start.17 = (f32[1024]{0:T(1024)S(1)}, f32[1024]{0:T(1024)}, u32[]{:S(2)}) copy-start(f32[1024]{0:T(1024)} %param.36) | copy-start | bytes 12292
  30.4 13.1 %copy-start.6 = (bf16[256,1024]{1,0:T(8,128)(2,1)S(1)}, bf16[256,1024]{1,0:T(8,128)(2,1)}, u32[]{:S(2)}) copy-start(bf16[256,1024]{1,0:T(8,128)(2,1)} %rest_9_.1) | copy-start | bytes 1572868
  35.2 9.3 %copy-start.7 = (bf16[1024,256]{1,0:T(8,128)(2,1)S(1)}, bf16[1024,256]{1,0:T(8,128)(2,1)}, u32[]{:S(2)}) copy-start(bf16[1024,256]{1,0:T(8,128)(2,1)} %rest_7_.1) | copy-start | bytes 1572868
  35.2 36.5 %collective-permute-start.3 = (bf16[14,48,128]{2,1,0:T(8,128)(2,1)}, bf16[14,48,128]{2,1,0:T(8,128)(2,1)}, u32[]{:S(2)}, u32[]{:S(2)}) collective-permute-start(bf16[14,48,128]{2,1,0:T(8,128)(2,1)} %get-tuple-element.19), channel_id=1, source_target_pairs={{0,7},{1,2},{2,1},{3,4},{4,3},{5,6},{6,5},{7,0},{8,15},{9,10},{10,... | collective-permute-start | bytes 516104 | tf_op jit(solution)/shard_map/ppermute | solution.py:49
  37.3 34.4 %collective-permute-start.2 = (bf16[14,48,128]{2,1,0:T(8,128)(2,1)}, bf16[14,48,128]{2,1,0:T(8,128)(2,1)}, u32[]{:S(2)}, u32[]{:S(2)}) collective-permute-start(bf16[14,48,128]{2,1,0:T(8,128)(2,1)} %get-tuple-element.19), channel_id=1, source_target_pairs={{0,1},{1,0},{2,3},{3,2},{4,5},{5,4},{6,7},{7,6},{8,9},{9,8},{10,11... | collective-permute-start | bytes 516104 | tf_op jit(solution)/shard_map/ppermute | solution.py:49
  41.5 4.0 %copy-start.15 = (f32[1536]{0:T(1024)S(1)}, f32[1536]{0:T(1024)}, u32[]{:S(2)}) copy-start(f32[1536]{0:T(1024)} %param.28) | copy-start | bytes 18436
  43.5 3.2 %copy-start = (bf16[384,1536]{1,0:T(8,128)(2,1)S(1)}, bf16[384,1536]{1,0:T(8,128)(2,1)}, u32[]{:S(2)}) copy-start(bf16[384,1536]{1,0:T(8,128)(2,1)} %rest_3_.1) | copy-start | bytes 3538948
  45.5 2.6 %copy-start.1 = (bf16[1536,384]{1,0:T(8,128)(2,1)S(1)}, bf16[1536,384]{1,0:T(8,128)(2,1)}, u32[]{:S(2)}) copy-start(bf16[1536,384]{1,0:T(8,128)(2,1)} %rest_1_.1) | copy-start | bytes 3538948
  66.1 3.9 %copy-start.9 = (bf16[2,8,16,128]{3,2,1,0:T(8,128)(2,1)S(1)}, bf16[2,8,16,128]{3,2,1,0:T(8,128)(2,1)}, u32[]{:S(2)}) copy-start(bf16[2,8,16,128]{3,2,1,0:T(8,128)(2,1)} %copy-done.8) | copy-start | bytes 196612
  112.1 5.3 %collective-permute-start.12 = (bf16[4,8,16,128]{3,2,1,0:T(8,128)(2,1)S(1)}, bf16[4,8,16,128]{3,2,1,0:T(8,128)(2,1)S(1)}, u32[]{:S(2)}, u32[]{:S(2)}) collective-permute-start(bf16[4,8,16,128]{3,2,1,0:T(8,128)(2,1)S(1)} %slice.19), channel_id=1, source_target_pairs={{0,1},{1,0},{2,3},{3,2},{4,5},{5,4},{6,7},{7,6},{8,9},{9,8},{10,11... | collective-permute-start | bytes 393224 | tf_op jit(solution)/shard_map/ppermute | solution.py:49
  112.2 12.8 %collective-permute-start.8 = (bf16[3,768,128]{2,1,0:T(8,128)(2,1)}, bf16[3,768,128]{2,1,0:T(8,128)(2,1)S(1)}, u32[]{:S(2)}, u32[]{:S(2)}) collective-permute-start(bf16[3,768,128]{2,1,0:T(8,128)(2,1)} %get-tuple-element.23), channel_id=1, source_target_pairs={{0,8},{8,0},{16,24},{24,16},{32,40},{40,32},{48,56},{56,48},{64,72... | collective-permute-start | bytes 1769480 | tf_op jit(solution)/shard_map/ppermute | solution.py:49
  112.3 13.2 %collective-permute-start.9 = (bf16[3,768,128]{2,1,0:T(8,128)(2,1)}, bf16[3,768,128]{2,1,0:T(8,128)(2,1)S(1)}, u32[]{:S(2)}, u32[]{:S(2)}) collective-permute-start(bf16[3,768,128]{2,1,0:T(8,128)(2,1)} %get-tuple-element.24), channel_id=1, source_target_pairs={{0,120},{8,16},{16,8},{24,32},{32,24},{40,48},{48,40},{56,64},{64,... | collective-permute-start | bytes 1769480 | tf_op jit(solution)/shard_map/ppermute | solution.py:49
  118.4 5.3 %collective-permute-start.13 = (bf16[2,8,16,128]{3,2,1,0:T(8,128)(2,1)S(1)}, bf16[2,8,16,128]{3,2,1,0:T(8,128)(2,1)S(1)}, u32[]{:S(2)}, u32[]{:S(2)}) collective-permute-start(bf16[2,8,16,128]{3,2,1,0:T(8,128)(2,1)S(1)} %slice.25), channel_id=1, source_target_pairs={{0,2},{1,3},{2,0},{3,1},{4,6},{5,7},{6,4},{7,5},{8,10},{9,11},{10,... | collective-permute-start | bytes 196616 | tf_op jit(solution)/shard_map/ppermute | solution.py:49
  123.7 10.2 %collective-permute-start.14 = (bf16[1,8,16,128]{3,2,1,0:T(8,128)(2,1)S(1)}, bf16[1,8,16,128]{3,2,1,0:T(8,128)(2,1)S(1)}, u32[]{:S(2)}, u32[]{:S(2)}) collective-permute-start(bf16[1,8,16,128]{3,2,1,0:T(8,128)(2,1)S(1)} %slice.27), channel_id=1, source_target_pairs={{0,4},{1,5},{2,6},{3,7},{4,0},{5,1},{6,2},{7,3},{8,12},{9,13},{10,... | collective-permute-start | bytes 98312 | tf_op jit(solution)/shard_map/ppermute | solution.py:49
  125.1 0.8 copy-start.4
  125.6 0.8 copy-start.5
  131.1 6.8 %collective-permute-start.11 = (bf16[14,48,128]{2,1,0:T(8,128)(2,1)}, bf16[14,48,128]{2,1,0:T(8,128)(2,1)S(1)}, u32[]{:S(2)}, u32[]{:S(2)}) collective-permute-start(bf16[14,48,128]{2,1,0:T(8,128)(2,1)} %get-tuple-element.26), channel_id=1, source_target_pairs={{0,7},{1,2},{2,1},{3,4},{4,3},{5,6},{6,5},{7,0},{8,15},{9,10},{10,... | collective-permute-start | bytes 516104 | tf_op jit(solution)/shard_map/ppermute | solution.py:49
  132.1 5.8 %collective-permute-start.10 = (bf16[14,48,128]{2,1,0:T(8,128)(2,1)}, bf16[14,48,128]{2,1,0:T(8,128)(2,1)S(1)}, u32[]{:S(2)}, u32[]{:S(2)}) collective-permute-start(bf16[14,48,128]{2,1,0:T(8,128)(2,1)} %get-tuple-element.26), channel_id=1, source_target_pairs={{0,1},{1,0},{2,3},{3,2},{4,5},{5,4},{6,7},{7,6},{8,9},{9,8},{10,11... | collective-permute-start | bytes 516104 | tf_op jit(solution)/shard_map/ppermute | solution.py:49
  133.9 4.0 %collective-permute-start.15 = (bf16[1,8,16,128]{3,2,1,0:T(8,128)(2,1)S(1)}, bf16[1,8,16,128]{3,2,1,0:T(8,128)(2,1)S(1)}, u32[]{:S(2)}, u32[]{:S(2)}) collective-permute-start(bf16[1,8,16,128]{3,2,1,0:T(8,128)(2,1)S(1)} %add_convert_fusion.2), channel_id=1, source_target_pairs={{0,128},{128,0},{1,129},{129,1},{2,130},{130,2},{3,131},{131,3},{4... | collective-permute-start | bytes 98312 | tf_op jit(solution)/shard_map/ppermute | solution.py:49
  137.9 0.6 copy-start.14
  138.0 0.7 copy-start.10
  138.0 0.7 copy-start.11
where the time goes:
time: 153 us; the launch traced here: 152 us
  Pallas kernels  84.6 us (55%)
  starting transfers between devices  28.2 us (18%)
  waiting for transfers between devices  18.6 us (12%)
  local copies, waits for them, and re-layouts  15.6 us (10%)
  other arithmetic  4.17 us (3%)
    ppermute x16, starting transfers between devices, swap(): return lax.ppermute(block, axes, route)  28.2 us
    pallas_call x1, Pallas kernels, cells(): pl.pallas_call(functools.partial(cells_kernel, models), in_specs=[VMEM, V...  26.3 us
    ppermute x16, waiting for transfers between devices, swap(): return lax.ppermute(block, axes, route)  18.6 us
    pallas_call x1, Pallas kernels, bands(): pl.pallas_call(bands_kernel, grid=(2, STEPS), in_specs=[pl.BlockSpec((1,...  14.1 us
    pallas_call x1, Pallas kernels, adjoint(): pl.pallas_call(functools.partial(adjoint_kernel, models), grid=(STEPS,),...  13.4 us
    pallas_call x1, Pallas kernels, mixing(): pl.pallas_call(functools.partial(mixing_kernel, models), grid=(STEPS,), i...  13.2 us
    pallas_call x2, Pallas kernels, gather_rows(): pl.pallas_call(gather_rows_kernel, grid=(stacked // 256,), in_specs=[pl.B...  9.58 us
    unnamed x62, local copies, waits for them, and re-layouts  8.07 us
  transfers between devices with their start and end apart: 16, of which 6 were waited for; matrix products, arithmetic and copies ran while one was open for 11% of the time, Pallas kernels for 18%

commit v1 on v0

v1 whole, which is shorter than its diff:
```python
import functools
import math

import jax
import jax.numpy as jnp
from jax import lax
from jax.experimental import pallas as pl
from jax.experimental.pallas import tpu as pltpu
from jax.sharding import PartitionSpec as P

KF = 16
EPS = 1e-06
INV_ROOT_TWO = 1.0 / math.sqrt(2.0)
NORMAL_PEAK = 1.0 / math.sqrt(2.0 * math.pi)
HALF_LOG2E = 0.5 * math.log2(math.e)
BF = jnp.bfloat16
F32 = jnp.float32
VMEM = pl.BlockSpec(memory_space=pltpu.VMEM)
SMEM = pl.BlockSpec(memory_space=pltpu.SMEM)
ANY = pl.BlockSpec(memory_space=pl.ANY)
STEPS = 8
ROWS = 8
LON = 128
TALL = 14


def params(**extra):
    return pltpu.CompilerParams(vmem_limit_bytes=56 * 2**20, **extra)


def cost(flops, nbytes):
    return pl.CostEstimate(flops=flops, bytes_accessed=nbytes, transcendentals=0)


def swap(block, axes, move):
    sizes = [lax.axis_size(axis) for axis in axes]
    route = []
    total = math.prod(sizes)
    for start in range(total):
        place = []
        rest = start
        for size in reversed(sizes):
            place.insert(0, rest % size)
            rest //= size
        goal = 0
        for size, value in zip(sizes, move(*place)):
            goal = goal * size + value
        route.append((start, goal))
    return lax.ppermute(block, axes, route)


def even_swap(block, axis):
    return swap(block, (axis,), lambda i: (i ^ 1,))


def odd_swap(block, axis):
    count = lax.axis_size(axis)
    return swap(block, (axis,), lambda i: ((((i + 1) ^ 1) - 1) % count,))


def model_keep(wet_ref):
    wet = wet_ref[...].astype(F32)
    return jnp.where(lax.axis_index("grid") == 1, wet, jnp.ones_like(wet))


def pack_outer(rows_ref, packed_ref, lots, base=0):
    lane = lax.broadcasted_iota(jnp.int32, (16, LON), 1)
    outer = (lane < 3) | (lane >= LON - 3)
    for row in range(ROWS):
        for lot in range(lots):
            total = jnp.zeros((16, LON), F32)
            for block in range(16):
                start = (lot * 16 + block) * 16
                values = rows_ref[row, start : start + 16, :].astype(F32)
                values = jnp.where(outer, values, 0.0)
                total = total + (pltpu.roll(values, 8 * block, 1) if block else values)
            packed_ref[row, lot * 16 : lot * 16 + 16, :] = total.astype(BF)


def prepare_kernel(
    field_ref, wet_ref, rows_ref, even_ref, odd_ref, surface_ref, packed_ref, scratch
):
    chans = field_ref.shape[0]
    keep = model_keep(wet_ref)
    held = field_ref[...].astype(F32) * keep[None]
    scratch[...] = held.reshape(chans * ROWS, LON)
    for row in range(ROWS):
        rows_ref[row] = scratch[pl.ds(row, chans, stride=ROWS), :].astype(BF)
    parity = lax.rem(lax.axis_index("lat"), 2)

    @pl.when(parity == 0)
    def _():
        even_ref[...] = rows_ref[ROWS - 3 :]
        odd_ref[...] = rows_ref[:3]

    @pl.when(parity == 1)
    def _():
        even_ref[...] = rows_ref[:3]
        odd_ref[...] = rows_ref[ROWS - 3 :]

    @pl.when(pl.program_id(0) == 0)
    def _():
        surface_ref[...] = rows_ref[:, :KF, :]

    pack_outer(rows_ref, packed_ref, 1)


def prepare(field, wet_mask):
    stacked = field.shape[0]
    part = 256
    return pl.pallas_call(
        prepare_kernel,
        grid=(stacked // part,),
        in_specs=[
            pl.BlockSpec((part, ROWS, LON), lambda s: (s, 0, 0)),
            pl.BlockSpec((ROWS, LON), lambda s: (0, 0)),
        ],
        out_specs=[
            pl.BlockSpec((ROWS, part, LON), lambda s: (0, s, 0)),
            pl.BlockSpec((3, part, LON), lambda s: (0, s, 0)),
            pl.BlockSpec((3, part, LON), lambda s: (0, s, 0)),
            pl.BlockSpec((ROWS, KF, LON), lambda s: (0, 0, 0)),
            pl.BlockSpec((ROWS, 16, LON), lambda s: (0, s, 0)),
        ],
        out_shape=[
            jax.ShapeDtypeStruct((ROWS, stacked, LON), BF),
            jax.ShapeDtypeStruct((3, stacked, LON), BF),
            jax.ShapeDtypeStruct((3, stacked, LON), BF),
            jax.ShapeDtypeStruct((ROWS, KF, LON), BF),
            jax.ShapeDtypeStruct((ROWS, stacked // 16, LON), BF),
        ],
        scratch_shapes=[pltpu.VMEM((part * ROWS, LON), F32)],
        compiler_params=params(),
        cost_estimate=cost(10**6, 5 * 10**6),
        name="prepare",
    )(field, wet_mask)


def ready_kernel(models, row_ref, *refs):
    inputs, refs = refs[:6], refs[6:]
    in_t_ref, out_t_ref, bias_ref, table_ref, taps_ref = refs

    def run(first, chans, w_in, w_out, kernel):
        units = w_out.shape[0]
        in_t_ref[:units, :chans] = w_in[...].T
        out_t_ref[:chans, :units] = w_out[...].T

        def column(start):
            return jnp.broadcast_to(row_ref[0:1, start : start + LON], (LON, LON)).T

        for start in range(0, units, LON):
            bias_ref[start : start + LON, :] = column(first + start)
        for k in range(4):
            for start in range(0, chans, LON):
                table_ref[k, start : start + LON, :] = column(first + units + k * chans + start)
        taken = kernel.shape[0]
        tap = lax.broadcasted_iota(jnp.int32, (taken, LON), 0)
        group = lax.broadcasted_iota(jnp.int32, (taken, LON), 1) // 16
        by_chan = jnp.transpose(kernel[...]).astype(BF)
        for col in range(7):
            for flip in range(2):
                wanted = (6 - group) * 7 + (6 - col) if flip else group * 7 + col
                pick = ((tap == wanted) & (group < 7)).astype(F32).astype(BF)
                spread = jnp.dot(by_chan, pick, preferred_element_type=F32)
                taps_ref[flip, col, :chans, :] = spread.astype(BF)

    first = 0
    for which, (chans, _) in enumerate(models):
        w_in, w_out, kernel = inputs[3 * which : 3 * which + 3]

        @pl.when(lax.axis_index("grid") == which)
        def _():
            run(first, chans, w_in, w_out, kernel)

        first += w_out.shape[0] + 4 * chans


def ready(models, rows, arrays):
    most = max(chans for chans, _ in models)
    units = max(arrays[1].shape[0], arrays[4].shape[0])
    return pl.pallas_call(
        functools.partial(ready_kernel, models),
        in_specs=[VMEM] * 7,
        out_specs=[VMEM] * 5,
        out_shape=[
            jax.ShapeDtypeStruct((units, most), BF),
            jax.ShapeDtypeStruct((most, units), BF),
            jax.ShapeDtypeStruct((units, LON), F32),
            jax.ShapeDtypeStruct((4, most, LON), F32),
            jax.ShapeDtypeStruct((2, 7, most, LON), BF),
        ],
        compiler_params=params(),
        cost_estimate=cost(10**9, 10 * 10**6),
        name="ready",
    )(jnp.concatenate(rows)[None], *arrays)


def cotangent_kernel(cot_ref, wet_ref, scale_ref, out_ref, scratch):
    chans = cot_ref.shape[0]
    keep = model_keep(wet_ref)
    held = cot_ref[...].astype(F32) * keep[None]
    scratch[...] = held.reshape(chans * ROWS, LON)
    scale = jnp.concatenate(
        [
            jnp.broadcast_to(scale_ref[0, 0:1, start : start + LON], (LON, LON)).T
            for start in range(0, chans, LON)
        ],
        axis=0,
    )
    for row in range(ROWS):
        out_ref[row] = (scale * scratch[pl.ds(row, chans, stride=ROWS), :]).astype(BF)


def scaled_cotangent(cot, wet_mask, scale_rows):
    stacked = cot.shape[0]
    part = 256
    return pl.pallas_call(
        cotangent_kernel,
        grid=(stacked // part,),
        in_specs=[
            pl.BlockSpec((part, ROWS, LON), lambda s: (s, 0, 0)),
            pl.BlockSpec((ROWS, LON), lambda s: (0, 0)),
            pl.BlockSpec((1, 1, part), lambda s: (s, 0, 0)),
        ],
        out_specs=pl.BlockSpec((ROWS, part, LON), lambda s: (0, s, 0)),
        out_shape=jax.ShapeDtypeStruct((ROWS, stacked, LON), BF),
        scratch_shapes=[pltpu.VMEM((part * ROWS, LON), F32)],
        compiler_params=params(),
        cost_estimate=cost(10**6, 4 * 10**6),
        name="scaled_cotangent",
    )(cot, wet_mask, scale_rows.reshape(stacked // part, 1, part))


def build_taps(taps_ref, chan_start, band_ref, slot):
    lane = lax.broadcasted_iota(jnp.int32, (16, LON), 1)
    chan = lax.broadcasted_iota(jnp.int32, (16, LON), 0)
    for col in range(7):
        values = taps_ref[col, pl.ds(chan_start, 16), :].astype(F32)
        kept = jnp.where(lax.rem(lane, 16) == chan, values, 0.0)
        band_ref[slot, col * 16 : col * 16 + 16, :] = kept.astype(BF)


def convolve(rows_ref, halo_ref, outer_ref, band_ref, slot, starts):
    lane = lax.broadcasted_iota(jnp.int32, (16, LON), 1)
    inner = []
    beyond = []
    for start in starts:
        place = pl.ds(pl.multiple_of(start, 16), 16)
        index = start // 16
        lot = pl.ds(pl.multiple_of((index // 16) * 16, 16), 16)
        turn = lax.rem(LON - 8 * lax.rem(index, 16), LON)
        inner.append(
            [halo_ref[row, place, :] for row in range(3)]
            + [rows_ref[row, place, :] for row in range(ROWS)]
            + [halo_ref[row, place, :] for row in range(3, 6)]
        )
        beyond.append(
            [pltpu.roll(outer_ref[row, lot, :], turn, 1).astype(BF) for row in range(TALL)]
        )
    count = len(starts)
    blank = jnp.zeros((16, 2 * count * LON), BF)
    wide = [
        jnp.concatenate([side[row] for side in inner + beyond], axis=1) for row in range(TALL)
    ] + [blank]
    band = band_ref[slot]
    totals = [[] for _ in starts]
    for row in range(ROWS):
        spread = jnp.concatenate(wide[row : row + 8], axis=0)
        terms = jnp.dot(band, spread, preferred_element_type=F32)
        for level in range(count):
            total = None
            for col in range(7):
                shift = col - 3
                here = slice(col * 16, col * 16 + 16)
                piece = terms[here, level * LON : (level + 1) * LON]
                if shift:
                    other = terms[here, (count + level) * LON : (count + level + 1) * LON]
                    edge = lane < shift if shift > 0 else lane >= LON + shift
                    piece = pltpu.roll(jnp.where(edge, other, piece), (-shift) % LON, 1)
                total = piece if total is None else total + piece
            totals[level].append(total)
    return [jnp.concatenate(total, axis=0) for total in totals]


def convolve_all(chans, levels, taps_ref, rows_ref, halo_ref, outer_ref, band_ref, finish):
    count = chans // 16 // STEPS

    def step(index, carry):
        bases = [pl.multiple_of((index * count + block) * 16, 16) for block in range(count)]
        for block, base in enumerate(bases):
            build_taps(taps_ref, base, band_ref, block)
        for block, base in enumerate(bases):
            starts = [base + level * chans for level in range(levels)]
            for start, total in zip(
                starts, convolve(rows_ref, halo_ref, outer_ref, band_ref, block, starts)
            ):
                finish(start, total)
        return carry

    lax.fori_loop(0, STEPS, step, 0)


def merge_outer(outer_in, corner_even, corner_odd, outer_ref):
    first, top_live, bottom_live = lat_place()
    for row in range(3):
        even = corner_even[row].astype(F32)
        odd = corner_odd[row].astype(F32)
        outer_ref[row] = jnp.where(first, odd, even) * top_live
        outer_ref[ROWS + 3 + row] = jnp.where(first, even, odd) * bottom_live
    for row in range(ROWS):
        outer_ref[3 + row] = outer_in[row].astype(F32)


def lat_place():
    lat = lax.axis_index("lat")
    top = (lat > 0).astype(F32)
    bottom = (lat < lax.axis_size("lat") - 1).astype(F32)
    return lax.rem(lat, 2) == 0, top, bottom


def halo_copies(even_ref, odd_ref, halo_ref, sems):
    odd_lat = lax.rem(lax.axis_index("lat"), 2)
    return [
        pltpu.make_async_copy(even_ref, halo_ref.at[pl.ds(3 - 3 * odd_lat, 3)], sems.at[0]),
        pltpu.make_async_copy(odd_ref, halo_ref.at[pl.ds(3 * odd_lat, 3)], sems.at[1]),
    ]


def blank_beyond(halo_ref):
    lat = lax.axis_index("lat")

    @pl.when(lat == 0)
    def _():
        halo_ref[:3] = jnp.zeros_like(halo_ref[:3])

    @pl.when(lat == lax.axis_size("lat") - 1)
    def _():
        halo_ref[3:] = jnp.zeros_like(halo_ref[3:])


def adjoint_kernel(
    models,
    rows_hbm,
    even_hbm,
    odd_hbm,
    outer_in,
    corner_even,
    corner_odd,
    taps_hbm,
    cot_hbm,
    wet_ref,
    first_ref,
    out_ref,
    rows_ref,
    halo_ref,
    taps_ref,
    cot_ref,
    outer_ref,
    band_ref,
    sems,
):
    copies = [
        pltpu.make_async_copy(rows_hbm, rows_ref, sems.at[2]),
        pltpu.make_async_copy(taps_hbm.at[1], taps_ref, sems.at[3]),
        pltpu.make_async_copy(cot_hbm, cot_ref, sems.at[4]),
    ] + halo_copies(even_hbm, odd_hbm, halo_ref, sems)
    for copy in copies:
        copy.start()
    merge_outer(outer_in, corner_even, corner_odd, outer_ref)
    keep = model_keep(wet_ref)
    for copy in copies:
        copy.wait()
    blank_beyond(halo_ref)

    def finish(start, total):
        place = pl.ds(pl.multiple_of(start, 16), 16)
        by_chan = jnp.swapaxes(total.reshape(ROWS, 16, LON), 0, 1)
        whole = cot_ref[place].astype(F32) * keep[None] + by_chan
        out_ref[place] = (whole * keep[None]).astype(BF)
        first_ref[jnp.where(jnp.asarray(start == 0), 0, 1)] = whole

    for which, (chans, levels) in enumerate(models):

        @pl.when(lax.axis_index("grid") == which)
        def _():
            convolve_all(
                chans, levels, taps_ref, rows_ref, halo_ref, outer_ref, band_ref, finish
            )


def conv_scratch(stacked, most):
    return [
        pltpu.VMEM((ROWS, stacked, LON), BF),
        pltpu.VMEM((6, stacked, LON), BF),
        pltpu.VMEM((7, most, LON), BF),
    ]


def adjoint(models, rows, even, odd, outer, corner_even, corner_odd, taps, cot, wet_mask):
    stacked = rows.shape[1]
    most = taps.shape[2]
    return pl.pallas_call(
        functools.partial(adjoint_kernel, models),
        in_specs=[ANY] * 3 + [VMEM] * 3 + [ANY] * 2 + [VMEM],
        out_specs=[VMEM, VMEM],
        out_shape=[
            jax.ShapeDtypeStruct((2, KF, ROWS, LON), F32),
            jax.ShapeDtypeStruct((stacked, ROWS, LON), BF),
        ],
        scratch_shapes=conv_scratch(stacked, most)
        + [
            pltpu.VMEM((stacked, ROWS, LON), BF),
            pltpu.VMEM((TALL, stacked // 16, LON), F32),
            pltpu.VMEM((3, 112, LON), BF),
            pltpu.SemaphoreType.DMA((5,)),
        ],
        compiler_params=params(),
        cost_estimate=cost(3 * 10**9, 8 * 10**6),
        name="adjoint",
    )(rows, even, odd, outer, corner_even, corner_odd, taps, cot, wet_mask)


def couple_kernel(first_ref, near_ref, far_ref, wet_ref, _, out_hbm, held_ref, sem):
    both = near_ref[...].astype(F32) + far_ref[...].astype(F32)
    keep = model_keep(wet_ref)
    held_ref[...] = ((first_ref[0] + jnp.swapaxes(both, 0, 1)) * keep[None]).astype(BF)
    copy = pltpu.make_async_copy(held_ref, out_hbm.at[pl.ds(0, KF)], sem)
    copy.start()
    copy.wait()


def couple(first, near, far, wet_mask, grads):
    return pl.pallas_call(
        couple_kernel,
        in_specs=[VMEM] * 4 + [ANY],
        out_specs=ANY,
        out_shape=jax.ShapeDtypeStruct(grads.shape, BF),
        input_output_aliases={4: 0},
        scratch_shapes=[pltpu.VMEM((KF, ROWS, LON), BF), pltpu.SemaphoreType.DMA],
        compiler_params=params(),
        cost_estimate=cost(10**5, 10**6),
        name="couple",
    )(first, near, far, wet_mask, grads)


def advance_kernel(rows_ref, wet_ref, out_ref):
    keep = model_keep(wet_ref)

    def turn(index, carry):
        place = pl.ds(pl.multiple_of(index * 16, 16), 16)
        by_chan = jnp.swapaxes(rows_ref[:, place, :].astype(F32), 0, 1)
        out_ref[place] = (by_chan * keep[None]).astype(BF)
        return carry

    lax.fori_loop(0, rows_ref.shape[1] // 16, turn, 0)


def advance(rows, wet_mask):
    stacked = rows.shape[1]
    part = 256
    return pl.pallas_call(
        advance_kernel,
        grid=(stacked // part,),
        in_specs=[
            pl.BlockSpec((ROWS, part, LON), lambda s: (0, s, 0)),
            pl.BlockSpec((ROWS, LON), lambda s: (0, 0)),
        ],
        out_specs=pl.BlockSpec((part, ROWS, LON), lambda s: (s, 0, 0)),
        out_shape=jax.ShapeDtypeStruct((stacked, ROWS, LON), BF),
        compiler_params=params(),
        cost_estimate=cost(10**6, 4 * 10**6),
        name="advance",
    )(rows, wet_mask)


def slot_of(source):
    apart = source ^ lax.axis_index("lon")
    far = apart >> 2
    return far | ((((apart >> 1) ^ far) & 1) << 1) | (((apart ^ far) & 1) << 2)


def cells_kernel(models, *refs):
    (
        rows_hbm,
        even_hbm,
        odd_hbm,
        outer_in,
        corner_even,
        corner_odd,
        taps_hbm,
        up_hbm,
        wet_ref,
        sources_ref,
        regrid_hbm,
        *refs,
    ) = refs
    pieces_hbm, refs = refs[:4], refs[4:]
    weights, refs = refs[:8], refs[8:]
    (advanced_hbm, grad_hbm, even_out, odd_out, packed_ref, *terms), refs = refs[:7], refs[7:]
    rows_ref, halo_ref, taps_ref, up_ref, regrid_ref, pieces_ref, outer_ref, band_ref = refs[:8]
    mixed_ref, forcing_ref, advanced_ref, grad_ref = refs[8:12]
    kept, refs = (refs[12:16], refs[16:20]), refs[20:]
    in_t_v, out_n_v, out_t_v, in_n_v, bias_v, table_v, sems, weight_sems = refs
    early = halo_copies(even_hbm, odd_hbm, halo_ref, sems) + [
        pltpu.make_async_copy(rows_hbm, rows_ref, sems.at[2]),
        pltpu.make_async_copy(taps_hbm.at[0], taps_ref, sems.at[3]),
    ]
    late = [
        pltpu.make_async_copy(src, dst, sems.at[4 + k])
        for k, (src, dst) in enumerate(
            [(up_hbm, up_ref), (regrid_hbm, regrid_ref)]
            + [
                (piece, pieces_ref.at[pl.ds(start, piece.shape[0])])
                for piece, start in zip(pieces_hbm, (0, 1, 2, 4))
            ]
        )
    ]
    for copy in early:
        copy.start()
    for copy in late:
        copy.start()
    merge_outer(outer_in, corner_even, corner_odd, outer_ref)
    for copy in early:
        copy.wait()
    blank_beyond(halo_ref)

    def mix(chans, levels):
        def finish(start, total):
            place = pl.ds(pl.multiple_of(start, 16), 16)
            for row in range(ROWS):
                mixed_ref[row, place, :] = total[row * 16 : row * 16 + 16]

        convolve_all(chans, levels, taps_ref, rows_ref, halo_ref, outer_ref, band_ref, finish)

    def force():
        for copy in late:
            copy.wait()
        slots = [slot_of(sources_ref[0, p]) for p in range(3)]
        for row in range(ROWS):
            total = None
            for p in range(3):
                part = lax.dot_general(
                    pieces_ref[slots[p], row],
                    regrid_ref[p, row],
                    (((1,), (1,)), ((), ())),
                    preferred_element_type=F32,
                )
                total = part if total is None else total + part
            forcing_ref[row] = total
        for ref in terms:
            ref[...] = jnp.zeros_like(ref)
        return slots

    def run(which, chans, levels):
        in_t, out_t, bias, table = weights[4:]
        in_n, out_n = weights[2 * which : 2 * which + 2]
        hidden_units = out_n.shape[0]
        units, wide_chans = pl.ds(0, hidden_units), pl.ds(0, chans)
        in_t_w, out_n_w = in_t_v.at[units, wide_chans], out_n_v.at[units, wide_chans]
        out_t_w, in_n_w = out_t_v.at[wide_chans, units], in_n_v.at[wide_chans, units]
        copies = [
            pltpu.make_async_copy(src, dst, weight_sems.at[k])
            for k, (src, dst) in enumerate(
                (
                    (in_t.at[units, wide_chans], in_t_w),
                    (out_n, out_n_w),
                    (out_t.at[wide_chans, units], out_t_w),
                    (in_n, in_n_w),
                    (bias, bias_v),
                    (table, table_v),
                )
            )
        ]
        for copy in copies:
            copy.start()
        gain_v, shift_v, bias_out_v, scale_v = [table_v.at[k, wide_chans] for k in range(4)]
        mix(chans, levels)
        slots = force()
        for copy in copies:
            copy.wait()
        share = 1.0 / chans
        wide = 2 * LON
        part = 256

        def pair(values):
            return jnp.concatenate([values, values], axis=1)

        def place_of(index):
            return lax.rem(index, 4) * 2, pl.ds(pl.multiple_of(index // 4 * chans, 16), chans)

        def front(index, slot):
            row, place = place_of(index)
            live = jnp.asarray(index < 4).astype(F32)
            act_ref, back_ref, unit_ref, inverse_ref = kept[slot]
            normed = []
            for k in range(2):
                mixed = mixed_ref[row + k, place, :]
                top = mixed[:KF] + forcing_ref[row + k] * live
                mixed = jnp.concatenate([top, mixed[KF:]], axis=0)
                centre = jnp.sum(mixed, axis=0, keepdims=True) * share
                spread = mixed - centre
                inverse = lax.rsqrt(jnp.sum(spread * spread, axis=0, keepdims=True) * share + EPS)
                unit = spread * inverse
                unit_ref[k, :chans, :] = unit
                inverse_ref[k] = jnp.broadcast_to(inverse, (8, LON))
                normed.append((unit * gain_v[...] + shift_v[...]).astype(BF))
            normed = jnp.concatenate(normed, axis=1)
            up = jnp.concatenate([up_ref[row, place, :], up_ref[row + 1, place, :]], axis=1)
            for start in range(0, hidden_units, part):
                these = slice(start, start + part)
                hidden = jnp.dot(in_t_w[these, :], normed, preferred_element_type=F32)
                active_grad = jnp.dot(out_n_w[these, :], up, preferred_element_type=F32)
                hidden = hidden + pair(bias_v[these, :])
                below = 0.5 + 0.5 * lax.erf(hidden * INV_ROOT_TWO)
                act_ref[these, :] = (hidden * below).astype(BF)
                bell = jnp.exp2((hidden * hidden) * -HALF_LOG2E) * NORMAL_PEAK
                back_ref[these, :] = (active_grad * (below + hidden * bell)).astype(BF)

        def back(index, slot):
            row, place = place_of(index)
            act_ref, back_ref, unit_ref, inverse_ref = kept[slot]
            update = jnp.dot(
                out_t_w[...], act_ref[:hidden_units, :], preferred_element_type=F32
            )
            normed_grad = jnp.dot(
                in_n_w[...], back_ref[:hidden_units, :], preferred_element_type=F32
            )
            for k in range(2):
                lanes = slice(k * LON, (k + 1) * LON)
                moved = scale_v[...] * (update[:, lanes] + bias_out_v[...])
                total = rows_ref[row + k, place, :].astype(F32) + moved
                advanced_ref[row + k, place, :] = total.astype(BF)
                scaled = normed_grad[:, lanes] * gain_v[...]
                unit = unit_ref[k, :chans, :]
                mean = jnp.sum(scaled, axis=0, keepdims=True) * share
                slope = jnp.sum(scaled * unit, axis=0, keepdims=True) * share
                inverse = inverse_ref[k, 0:1, :]
                grad_ref[row + k, place, :] = (inverse * (scaled - mean - unit * slope)).astype(BF)

        count = levels * 4
        front(0, 0)

        def turn(index, carry):
            front(2 * index + 1, 1)
            back(2 * index, 0)
            front(2 * index + 2, 0)
            back(2 * index + 1, 1)
            return carry

        lax.fori_loop(0, count // 2 - 1, turn, 0)
        front(count - 1, 1)
        back(count - 2, 0)
        back(count - 1, 1)
        for row in range(ROWS):
            for p in range(3):
                term = jnp.dot(
                    grad_ref[row, :KF, :], regrid_ref[p, row], preferred_element_type=F32
                ).astype(BF)
                for side, ref in enumerate(terms):

                    @pl.when(slots[p] // 4 == side)
                    def _():
                        ref[lax.rem(slots[p], 4), row] = term

    for which, (chans, levels) in enumerate(models):

        @pl.when(lax.axis_index("grid") == which)
        def _():
            run(which, chans, levels)

    odd_lat = lax.rem(lax.axis_index("lat"), 2)
    lower = ROWS - 3
    leaving = [
        pltpu.make_async_copy(grad_ref.at[pl.ds(lower * (1 - odd_lat), 3)], even_out, sems.at[0]),
        pltpu.make_async_copy(grad_ref.at[pl.ds(lower * odd_lat, 3)], odd_out, sems.at[1]),
        pltpu.make_async_copy(grad_ref, grad_hbm, sems.at[2]),
        pltpu.make_async_copy(advanced_ref, advanced_hbm, sems.at[3]),
    ]
    for copy in leaving:
        copy.start()
    pack_outer(grad_ref, packed_ref, grad_ref.shape[1] // 256)
    for copy in leaving:
        copy.wait()


def cells(
    models,
    rows,
    even,
    odd,
    outer,
    corner_even,
    corner_odd,
    taps,
    up,
    wet_mask,
    sources,
    regrid,
    pieces,
    weights,
):
    stacked = rows.shape[1]
    most_chans = max(chans for chans, _ in models)
    most_units = weights[4].shape[0]
    return pl.pallas_call(
        functools.partial(cells_kernel, models),
        in_specs=[ANY] * 3
        + [VMEM] * 3
        + [ANY] * 2
        + [VMEM, SMEM]
        + [ANY] * (1 + 4 + 8),
        out_specs=[ANY] * 4 + [VMEM] * 3,
        out_shape=[
            jax.ShapeDtypeStruct((ROWS, stacked, LON), BF),
            jax.ShapeDtypeStruct((ROWS, stacked, LON), BF),
            jax.ShapeDtypeStruct((3, stacked, LON), BF),
            jax.ShapeDtypeStruct((3, stacked, LON), BF),
            jax.ShapeDtypeStruct((ROWS, stacked // 16, LON), BF),
            jax.ShapeDtypeStruct((4, ROWS, KF, LON), BF),
            jax.ShapeDtypeStruct((4, ROWS, KF, LON), BF),
        ],
        scratch_shapes=conv_scratch(stacked, taps.shape[2])
        + [
            pltpu.VMEM(up.shape, BF),
            pltpu.VMEM(regrid.shape, BF),
            pltpu.VMEM((8, ROWS, KF, LON), BF),
            pltpu.VMEM((TALL, stacked // 16, LON), F32),
            pltpu.VMEM((3, 112, LON), BF),
            pltpu.VMEM((ROWS, stacked, LON), F32),
            pltpu.VMEM((ROWS, KF, LON), F32),
            pltpu.VMEM((ROWS, stacked, LON), BF),
            pltpu.VMEM((ROWS, stacked, LON), BF),
        ]
        + [
            pltpu.VMEM((most_units, 2 * LON), BF),
            pltpu.VMEM((most_units, 2 * LON), BF),
            pltpu.VMEM((2, most_chans, LON), F32),
            pltpu.VMEM((2, 8, LON), F32),
        ]
        * 2
        + [
            pltpu.VMEM((most_units, most_chans), BF),
            pltpu.VMEM((most_units, most_chans), BF),
            pltpu.VMEM((most_chans, most_units), BF),
            pltpu.VMEM((most_chans, most_units), BF),
            pltpu.VMEM((most_units, LON), F32),
            pltpu.VMEM((4, most_chans, LON), F32),
            pltpu.SemaphoreType.DMA((10,)),
            pltpu.SemaphoreType.DMA((6,)),
        ],
        compiler_params=params(),
        cost_estimate=cost(10**10, 20 * 10**6),
        name="cells",
    )(
        rows,
        even,
        odd,
        outer,
        corner_even,
        corner_odd,
        taps,
        up,
        wet_mask,
        sources,
        regrid,
        *pieces,
        *weights,
    )


def swap_outer(packed):
    first = lax.rem(lax.axis_index("lon"), 2) == 0
    east_west = [even_swap(packed, "lon"), odd_swap(packed, "lon")]
    lane = lax.broadcasted_iota(jnp.int32, packed.shape, 2)
    from_even = (lax.rem(lane, 8) < 4) == first
    outer = jnp.where(from_even, *east_west)
    north = lax.rem(lax.axis_index("lat"), 2) == 1
    ends = (outer[:3], outer[ROWS - 3 :])
    even = even_swap(jnp.where(north, ends[0], ends[1]), "lat")
    odd = odd_swap(jnp.where(north, ends[1], ends[0]), "lat")
    return outer, even, odd


def cross(block, apart):
    return swap(block, ("grid", "lon"), lambda g, j: (1 - g, j ^ apart))


def lon_swap(block, apart):
    return swap(block, ("lon",), lambda j: (j ^ apart,))


def per_device(
    fields,
    cotangent,
    wet_mask,
    atmos_kernel,
    atmos_gain,
    atmos_shift,
    atmos_w_in,
    atmos_b_in,
    atmos_w_out,
    atmos_b_out,
    atmos_scale,
    ocean_kernel,
    ocean_gain,
    ocean_shift,
    ocean_w_in,
    ocean_b_in,
    ocean_w_out,
    ocean_b_out,
    ocean_scale,
    sources,
    regrid,
):
    stacked = fields.shape[1]
    models = tuple((w.shape[0], stacked // w.shape[0]) for w in (atmos_w_in, ocean_w_in))
    is_ocean = lax.axis_index("grid") == 1
    field, cot = fields[0], cotangent[0]
    rows, even, odd, surface, packed = prepare(field, wet_mask)
    pieces = [cross(surface[None], 0), cross(surface[None], 7)]
    around = swap_outer(packed)
    even = even_swap(even, "lat")
    odd = odd_swap(odd, "lat")
    scale_rows = jnp.where(
        is_ocean,
        jnp.tile(ocean_scale, models[1][1]),
        jnp.tile(atmos_scale, models[0][1]),
    )
    up = scaled_cotangent(cot, wet_mask, scale_rows[:, None])
    pieces.append(lon_swap(jnp.concatenate(pieces, axis=0), 2))
    *pieces, up = lax.optimization_barrier((*pieces, up))
    pieces.append(lon_swap(jnp.concatenate(pieces, axis=0), 1))
    made = ready(
        models,
        (
            atmos_b_in,
            atmos_gain,
            atmos_shift,
            atmos_b_out,
            atmos_scale,
            ocean_b_in,
            ocean_gain,
            ocean_shift,
            ocean_b_out,
            ocean_scale,
        ),
        (
            atmos_w_in,
            atmos_w_out,
            atmos_kernel.T,
            ocean_w_in,
            ocean_w_out,
            ocean_kernel.T,
        ),
    )
    around, pieces, made = lax.optimization_barrier((around, pieces, made))
    in_t, out_t, bias, table, taps = made
    weights = [atmos_w_in, atmos_w_out, ocean_w_in, ocean_w_out, in_t, out_t, bias, table]
    advanced, grad, even, odd, packed, near, far = cells(
        models,
        rows,
        even,
        odd,
        *around,
        taps,
        up,
        wet_mask,
        sources[0, 0],
        regrid[0, 0, 0],
        pieces,
        weights,
    )
    came = lon_swap(far, 1)
    around = swap_outer(packed)
    even = even_swap(even, "lat")
    odd = odd_swap(odd, "lat")
    sums = [(near[k : k + 2].astype(F32) + came[k : k + 2].astype(F32)) for k in (0, 2)]
    came = lon_swap(sums[1].astype(BF), 2)
    advanced = advance(advanced, wet_mask)
    came, advanced = lax.optimization_barrier((came, advanced))
    ends = [(sums[0][k] + came[k].astype(F32)).astype(BF) for k in range(2)]
    coupling = cross(ends[0], 0), cross(ends[1], 7)
    first, field_grads = adjoint(models, grad, even, odd, *around, taps, cot, wet_mask)
    field_grads = couple(first, *coupling, wet_mask, field_grads)
    return (advanced[None], field_grads[None])


def solution(mesh):
    placed = (
        (P("grid", None, "lat", "lon"),) * 2
        + (P("lat", "lon"),)
        + (P(),) * 16
        + (P("grid", "lat", "lon", None), P("grid", "lat", "lon", None, None, None, None))
    )
    return jax.shard_map(
        per_device,
        mesh=mesh,
        in_specs=placed,
        out_specs=(P("grid", None, "lat", "lon"), P("grid", None, "lat", "lon")),
        check_vma=False,
    )
```

time: 153 us -> 111 us (0.73)
  Pallas kernels: 84.6 us -> 64.5 us
  local copies, waits for them, and re-layouts: 15.6 us -> 2.79 us
  waiting for transfers between devices: 18.6 us -> 10.7 us
  other arithmetic: 4.17 us -> 0.72 us
    pallas_call x7 -> x6, Pallas kernels: 80.5 us -> 60 us  [the longest x1 32 us: cells(): pl.pallas_call(functools.partial(cells_kernel, models), in_specs=[ANY] *...]
    ppermute x16 -> x20, waiting for transfers between devices: 18.6 us -> 10.7 us  [swap(): return lax.ppermute(block, axes, route)]
    unnamed x62 -> x67, local copies, waits for them, and re-layouts: 8.07 us -> 2.77 us
    broadcast_in_dim x3 -> x0, local copies, waits for them, and re-layouts: 2.44 us -> none  [the longest x2 2.23 us: per_device(): b_in[:, None]]
    reshape x2 -> x0, local copies, waits for them, and re-layouts: 2.35 us -> none  [the longest x1 2.23 us: per_device(): taps = jnp.repeat(both, 16, axis=3)]
    concatenate x3 -> x2, other arithmetic: 2.31 us -> 0.02 us  [the longest x1 0.02 us: per_device(): pieces.append(lon_swap(jnp.concatenate(pieces, axis=0), 1))]
    another operation x8 -> x2, local copies, waits for them, and re-layouts: 1.66 us -> 0.02 us  [per_device(): jnp.tile(atmos_scale, models[0][1])]
    ppermute x16 -> x20, starting transfers between devices: 28.2 us -> 28.7 us  [swap(): return lax.ppermute(block, axes, route)]
  transfers between devices with their start and end apart: 16 -> 20, of which waited for: 6 -> 4; matrix products, arithmetic and copies ran while one was open for 11% -> 1% of each run, Pallas kernels for 18% -> 24%
where the time goes in v1:
time: 111 us; the launch traced here: 109 us
  Pallas kernels  64.5 us (58%)
  starting transfers between devices  28.7 us (26%)
  waiting for transfers between devices  10.7 us (10%)
  local copies, waits for them, and re-layouts  2.79 us (3%)
  between operations  1.35 us (1%)
    pallas_call x1, Pallas kernels, cells(): pl.pallas_call(functools.partial(cells_kernel, models), in_specs=[ANY] *...  32 us
    ppermute x20, starting transfers between devices, swap(): return lax.ppermute(block, axes, route)  28.7 us
    pallas_call x1, Pallas kernels, adjoint(): pl.pallas_call(functools.partial(adjoint_kernel, models), in_specs=[ANY]...  13.2 us
    ppermute x20, waiting for transfers between devices, swap(): return lax.ppermute(block, axes, route)  10.7 us
    pallas_call x1, Pallas kernels, ready(): pl.pallas_call(functools.partial(ready_kernel, models), in_specs=[VMEM] *...  5.54 us
    pallas_call x1, Pallas kernels, prepare(): pl.pallas_call(prepare_kernel, grid=(stacked // part,), in_specs=[pl.Bloc...  4.42 us
    pallas_call x1, Pallas kernels, advance(): pl.pallas_call(advance_kernel, grid=(stacked // part,), in_specs=[pl.Bloc...  3.86 us
    pallas_call x1, Pallas kernels, scaled_cotangent(): pl.pallas_call(cotangent_kernel, grid=(stacked // part,), in_specs=[pl.Bl...  3.84 us
  transfers between devices with their start and end apart: 20, of which 4 were waited for; matrix products, arithmetic and copies ran while one was open for 1% of the time, Pallas kernels for 24%

profile of v1, /device:TPU:32, one launch (start us, length us, event | category | flops | bytes accessed | tf_op | source)
XLA Modules:
  0.0 108.7 jit_solution(11289541863781329642)
XLA Ops:
  0.7 4.4 %prepare.1 = (bf16[8,768,128]{2,1,0:T(8,128)(2,1)}, bf16[3,768,128]{2,1,0:T(8,128)(2,1)}, bf16[3,768,128]{2,1,0:T(8,128)(2,1)}, bf16[8,16,128]{2,1,0:T(8,128)(2,1)}, bf16[8,48,128]{2,1,0:T(8,128)(2,1)}) custom-call(bf16[768,8,128]{2,1,0:T(8,128)(2,1)} %bitcast.14, s32[8,128]{1,0:T(8,128)} %wet_ref.9), custom_call_target="tpu_custom_call" | custom-call | flops 1000000 | bytes 5000000 | tf_op jit(solution)/shard_map/prepare/pallas_call | solution.py:111
  5.2 6.9 %collective-permute-start.7 = (bf16[1,8,16,128]{3,2,1,0:T(8,128)(2,1)}, bf16[1,8,16,128]{3,2,1,0:T(8,128)(2,1)S(1)}, u32[]{:S(2)}, u32[]{:S(2)}) collective-permute-start(bf16[1,8,16,128]{3,2,1,0:T(8,128)(2,1)} %bitcast.22), channel_id=1, source_target_pairs={{0,135},{1,134},{2,133},{3,132},{4,131},{5,130},{6,129},{7,128},{1... | collective-permute-start | bytes 98312 | tf_op jit(solution)/shard_map/ppermute | solution.py:49
  12.1 0.5 collective-permute-start.6
  12.5 1.0 collective-permute-start.3
  13.6 0.0 collective-permute-start.2
  13.6 0.0 collective-permute-start
  13.6 0.0 copy-done.9
  13.7 0.0 copy-done.15
  13.8 0.0 copy-done.17
  13.8 0.6 broadcast_select_fusion.6.scale_ref
  14.4 3.8 %scaled_cotangent.1.refs_7_ = bf16[8,768,128]{2,1,0:T(8,128)(2,1)} custom-call(bf16[768,8,128]{2,1,0:T(8,128)(2,1)} %bitcast.15, s32[8,128]{1,0:T(8,128)} %wet_ref.9, f32[3,1,256]{2,1,0:T(1,128)} %broadcast_select_fusion.6.scale_ref), custom_call_target="tpu_custom_call" | custom-call | flops 1000000 | bytes 4000000 | tf_op jit(solution)/shard_map/scaled_cotangent/pallas_call | solution.py:217
  18.2 0.0 collective-permute-done.7.refs_12_
  18.3 5.6 %collective-permute-start.1 = (bf16[3,768,128]{2,1,0:T(8,128)(2,1)S(1)}, bf16[3,768,128]{2,1,0:T(8,128)(2,1)S(1)}, u32[]{:S(2)}, u32[]{:S(2)}) collective-permute-start(bf16[3,768,128]{2,1,0:T(8,128)(2,1)S(1)} %copy-done.18), channel_id=1, source_target_pairs={{0,120},{8,16},{16,8},{24,32},{32,24},{40,48},{48,40},{56,64},{64,... | collective-permute-start | bytes 1769480 | tf_op jit(solution)/shard_map/ppermute | solution.py:49
  23.8 0.0 collective-permute-done.6.refs_11_
  23.9 2.6 %collective-permute-start.8 = (bf16[2,8,16,128]{3,2,1,0:T(8,128)(2,1)S(1)}, bf16[2,8,16,128]{3,2,1,0:T(8,128)(2,1)S(1)}, u32[]{:S(2)}, u32[]{:S(2)}) collective-permute-start(bf16[2,8,16,128]{3,2,1,0:T(8,128)(2,1)S(1)} %pad_maximum_fusion.1), channel_id=1, source_target_pairs={{0,2},{1,3},{2,0},{3,1},{4,6},{5,7},{6,4},{7,5},{8,10},{9,11},{10,... | collective-permute-start | bytes 196616 | tf_op jit(solution)/shard_map/ppermute | solution.py:49
  26.4 3.3 %collective-permute-done.8.refs_13_ = bf16[2,8,16,128]{3,2,1,0:T(8,128)(2,1)S(1)} collective-permute-done((bf16[2,8,16,128]{3,2,1,0:T(8,128)(2,1)S(1)}, bf16[2,8,16,128]{3,2,1,0:T(8,128)(2,1)S(1)}, u32[]{:S(2)}, u32[]{:S(2)}) %collective-permute-start.8) | collective-permute-done | bytes 65568 | tf_op jit(solution)/shard_map/ppermute | solution.py:49
  29.8 1.9 %collective-permute-start.9 = (bf16[4,8,16,128]{3,2,1,0:T(8,128)(2,1)S(1)}, bf16[4,8,16,128]{3,2,1,0:T(8,128)(2,1)S(1)}, u32[]{:S(2)}, u32[]{:S(2)}) collective-permute-start(bf16[4,8,16,128]{3,2,1,0:T(8,128)(2,1)S(1)} %pad_maximum_fusion), channel_id=1, source_target_pairs={{0,1},{1,0},{2,3},{3,2},{4,5},{5,4},{6,7},{7,6},{8,9},{9,8},{10,11... | collective-permute-start | bytes 393224 | tf_op jit(solution)/shard_map/ppermute | solution.py:49
  31.6 0.0 collective-permute-done.3
  31.6 0.0 collective-permute-done.2
  31.7 0.0 copy-start.1
  31.7 0.1 collective-permute-start.5
  31.8 0.1 collective-permute-start.4
  31.9 5.5 %ready.1 = (bf16[1536,384]{1,0:T(8,128)(2,1)}, bf16[384,1536]{1,0:T(8,128)(2,1)}, f32[1536,128]{1,0:T(8,128)}, f32[4,384,128]{2,1,0:T(8,128)}, bf16[2,7,384,128]{3,2,1,0:T(8,128)(2,1)}) custom-call(f32[1,5120]{1,0:T(1,128)} %bitcast.24, bf16[384,1536]{1,0:T(8,128)(2,1)} %refs_15_.1, bf16[1536,384]{1,0:T(8,128)(2,1)} %refs_16_.1, f32[49,384]{1,0:T(8,128)} %bitcast.20, ...), custom_call_target="tpu_custom_call" | custom-call | flops 1000000000 | bytes 10000000 | tf_op jit(solution)/shard_map/ready/pallas_call | solution.py:181
  37.4 0.0 copy-done.5
  37.5 1.3 %collective-permute-done.5.refs_5_ = bf16[3,48,128]{2,1,0:T(8,128)(2,1)S(1)} collective-permute-done((bf16[3,48,128]{2,1,0:T(8,128)(2,1)S(1)}, bf16[3,48,128]{2,1,0:T(8,128)(2,1)S(1)}, u32[]{:S(2)}, u32[]{:S(2)}) %collective-permute-start.5) | collective-permute-done | bytes 36896 | tf_op jit(solution)/shard_map/ppermute | solution.py:49
  38.8 0.0 collective-permute-done.4.refs_4_
  38.8 0.0 collective-permute-done.9.refs_14_
  38.8 0.0 collective-permute-done.refs_1_
  38.8 0.0 collective-permute-done.1.refs_2_
  38.8 0.5 copy-done.24
  39.4 0.0 copy-done.26
  39.4 0.0 copy-done.23
  39.4 0.2 copy-done.19
  39.7 0.2 copy-done.20
  39.9 32.0 %cells.1 = (bf16[8,768,128]{2,1,0:T(8,128)(2,1)}, bf16[8,768,128]{2,1,0:T(8,128)(2,1)}, bf16[3,768,128]{2,1,0:T(8,128)(2,1)}, bf16[3,768,128]{2,1,0:T(8,128)(2,1...) custom-call(bf16[8,768,128]{2,1,0:T(8,128)(2,1)} %get-tuple-element.39.refs_0_, ...), custom_call_target="tpu_custom_call" | custom-call | flops 10000000000 | bytes 20000000 | tf_op jit(solution)/shard_map/cells/pallas_call | solution.py:705
  71.9 1.1 %collective-permute-start.15 = (bf16[8,48,128]{2,1,0:T(8,128)(2,1)}, bf16[8,48,128]{2,1,0:T(8,128)(2,1)S(1)}, u32[]{:S(2)}, u32[]{:S(2)}) collective-permute-start(bf16[8,48,128]{2,1,0:T(8,128)(2,1)} %get-tuple-element.72), channel_id=1, source_target_pairs={{0,7},{1,2},{2,1},{3,4},{4,3},{5,6},{6,5},{7,0},{8,15},{9,10},{10,... | collective-permute-start | bytes 294920 | tf_op jit(solution)/shard_map/ppermute | solution.py:49
  73.0 1.1 %collective-permute-start.14 = (bf16[8,48,128]{2,1,0:T(8,128)(2,1)}, bf16[8,48,128]{2,1,0:T(8,128)(2,1)S(1)}, u32[]{:S(2)}, u32[]{:S(2)}) collective-permute-start(bf16[8,48,128]{2,1,0:T(8,128)(2,1)} %get-tuple-element.72), channel_id=1, source_target_pairs={{0,1},{1,0},{2,3},{3,2},{4,5},{5,4},{6,7},{7,6},{8,9},{9,8},{10,11... | collective-permute-start | bytes 294920 | tf_op jit(solution)/shard_map/ppermute | solution.py:49
  74.1 0.9 collective-permute-start.10
  75.0 0.0 collective-permute-start.12
  75.0 4.2 %collective-permute-start.13 = (bf16[3,768,128]{2,1,0:T(8,128)(2,1)}, bf16[3,768,128]{2,1,0:T(8,128)(2,1)S(1)}, u32[]{:S(2)}, u32[]{:S(2)}) collective-permute-start(bf16[3,768,128]{2,1,0:T(8,128)(2,1)} %get-tuple-element.71), channel_id=1, source_target_pairs={{0,120},{8,16},{16,8},{24,32},{32,24},{40,48},{48,40},{56,64},{64,... | collective-permute-start | bytes 1769480 | tf_op jit(solution)/shard_map/ppermute | solution.py:49
  79.2 3.9 %advance.1 = bf16[768,8,128]{2,1,0:T(8,128)(2,1)} custom-call(bf16[8,768,128]{2,1,0:T(8,128)(2,1)} %get-tuple-element.67.rows_ref, s32[8,128]{1,0:T(8,128)} %wet_ref.9), custom_call_target="tpu_custom_call" | custom-call | flops 1000000 | bytes 4000000 | tf_op jit(solution)/shard_map/advance/pallas_call | solution.py:461
  83.1 0.0 collective-permute-done.15
  83.1 0.0 collective-permute-done.14
  83.1 0.0 collective-permute-done.10
  83.2 1.7 %collective-permute-start.11 = (bf16[2,8,16,128]{3,2,1,0:T(8,128)(2,1)S(1)}, bf16[2,8,16,128]{3,2,1,0:T(8,128)(2,1)S(1)}, u32[]{:S(2)}, u32[]{:S(2)}) collective-permute-start(bf16[2,8,16,128]{3,2,1,0:T(8,128)(2,1)S(1)} %get-tuple-element.77), channel_id=1, source_target_pairs={{0,2},{1,3},{2,0},{3,1},{4,6},{5,7},{6,4},{7,5},{8,10},{9,11},{10,... | collective-permute-start | bytes 196616 | tf_op jit(solution)/shard_map/ppermute | solution.py:49
  84.9 1.0 collective-permute-start.17
  85.9 0.0 collective-permute-start.16
  85.9 2.7 %collective-permute-done.11 = bf16[2,8,16,128]{3,2,1,0:T(8,128)(2,1)S(1)} collective-permute-done((bf16[2,8,16,128]{3,2,1,0:T(8,128)(2,1)S(1)}, bf16[2,8,16,128]{3,2,1,0:T(8,128)(2,1)S(1)}, u32[]{:S(2)}, u32[]{:S(2)}) %collective-permute-start.11) | collective-permute-done | bytes 65568 | tf_op jit(solution)/shard_map/ppermute | solution.py:49
  88.5 0.1 collective-permute-start.19
  88.6 3.3 %collective-permute-done.17.corner_odd = bf16[3,48,128]{2,1,0:T(8,128)(2,1)S(1)} collective-permute-done((bf16[3,48,128]{2,1,0:T(8,128)(2,1)S(1)}, bf16[3,48,128]{2,1,0:T(8,128)(2,1)S(1)}, u32[]{:S(2)}, u32[]{:S(2)}) %collective-permute-start.17) | collective-permute-done | bytes 36896 | tf_op jit(solution)/shard_map/ppermute | solution.py:49
  92.0 0.0 collective-permute-start.18
  92.0 0.0 collective-permute-done.16.corner_even
  92.0 0.0 collective-permute-done.12.even_hbm
  92.0 0.0 collective-permute-done.13.odd_hbm
  92.0 0.5 copy-done.25
  92.6 0.0 copy-done.27
  92.6 0.2 copy-done.21
  92.8 0.2 copy-done.22
  93.0 13.2 %adjoint.1 = (f32[2,16,8,128]{3,2,1,0:T(8,128)}, bf16[768,8,128]{2,1,0:T(8,128)(2,1)}) custom-call(bf16[8,768,128]{2,1,0:T(8,128)(2,1)} %get-tuple-element.69.rows_hbm, bf16[3,768,128]{2,1,0:T(8,128)(2,1)} %copy-done.21, bf16[3,768,128]{2,1,0:T(8,128)(2,1)} %copy-done.22, bf16[8,48,128]{2,1,0:T(8,128)(2,1)} %copy-done, bf16[3,48,128]{2,1,0:T(8,128)(2,1)} %copy-done.27, ...), custom_call_target="tpu_custom_call" | custom-call | flops 3000000000 | bytes 8000000 | tf_op jit(solution)/shard_map/adjoint/pallas_call | solution.py:402
  106.3 0.0 collective-permute-done.19.far_ref
  106.3 0.0 collective-permute-done.18.near_ref
  106.3 0.6 copy-done.6
  106.9 0.0 copy-done.7
  106.9 1.6 %couple.1 = bf16[768,8,128]{2,1,0:T(8,128)(2,1)} custom-call(f32[2,16,8,128]{3,2,1,0:T(8,128)} %get-tuple-element.73.first_ref, bf16[8,16,128]{2,1,0:T(8,128)(2,1)} %copy-done.7, bf16[8,16,128]{2,1,0:T(8,128)(2,1)} %copy-done.6, s32[8,128]{1,0:T(8,128)} %wet_ref.9, bf16[768,8,128]{2,1,0:T(8,128)(2,1)} %get-tuple-element.75._), custom_call_target="tpu_custom_call", output_to_operand_aliasing={{}: (4, {})} | custom-call | flops 100000 | bytes 1000000 | tf_op jit(solution)/shard_map/couple/pallas_call | solution.py:433
  (64 shorter events, 0.3 us)
Async XLA Ops:
  0.6 12.9 %copy-start.9 = (f32[384]{0:T(512)S(1)}, f32[384]{0:T(512)}, u32[]{:S(2)}) copy-start(f32[384]{0:T(512)} %param.31) | copy-start | bytes 4612
  0.6 13.0 %copy-start.8 = (f32[1536]{0:T(1024)S(1)}, f32[1536]{0:T(1024)}, u32[]{:S(2)}) copy-start(f32[1536]{0:T(1024)} %param.28) | copy-start | bytes 18436
  0.7 13.0 %copy-start.12 = (f32[384]{0:T(512)S(1)}, f32[384]{0:T(512)}, u32[]{:S(2)}) copy-start(f32[384]{0:T(512)} %param.25) | copy-start | bytes 4612
  0.7 13.0 %copy-start.13 = (f32[384]{0:T(512)S(1)}, f32[384]{0:T(512)}, u32[]{:S(2)}) copy-start(f32[384]{0:T(512)} %param.26) | copy-start | bytes 4612
  0.7 13.0 %copy-start.14 = (f32[384]{0:T(512)S(1)}, f32[384]{0:T(512)}, u32[]{:S(2)}) copy-start(f32[384]{0:T(512)} %param.30) | copy-start | bytes 4612
  0.7 13.0 %copy-start.11 = (f32[1024]{0:T(1024)S(1)}, f32[1024]{0:T(1024)}, u32[]{:S(2)}) copy-start(f32[1024]{0:T(1024)} %param.36) | copy-start | bytes 12292
  0.7 13.0 %copy-start.15 = (f32[256]{0:T(256)S(1)}, f32[256]{0:T(256)}, u32[]{:S(2)}) copy-start(f32[256]{0:T(256)} %param.33) | copy-start | bytes 3076
  0.7 13.0 %copy-start.16 = (f32[256]{0:T(256)S(1)}, f32[256]{0:T(256)}, u32[]{:S(2)}) copy-start(f32[256]{0:T(256)} %param.34) | copy-start | bytes 3076
  0.7 13.1 %copy-start.17 = (f32[256]{0:T(256)S(1)}, f32[256]{0:T(256)}, u32[]{:S(2)}) copy-start(f32[256]{0:T(256)} %param.38) | copy-start | bytes 3076
  0.7 13.1 %copy-start.10 = (f32[256]{0:T(256)S(1)}, f32[256]{0:T(256)}, u32[]{:S(2)}) copy-start(f32[256]{0:T(256)} %param.39) | copy-start | bytes 3076
  5.2 13.1 %collective-permute-start.7 = (bf16[1,8,16,128]{3,2,1,0:T(8,128)(2,1)}, bf16[1,8,16,128]{3,2,1,0:T(8,128)(2,1)S(1)}, u32[]{:S(2)}, u32[]{:S(2)}) collective-permute-start(bf16[1,8,16,128]{3,2,1,0:T(8,128)(2,1)} %bitcast.22), channel_id=1, source_target_pairs={{0,135},{1,134},{2,133},{3,132},{4,131},{5,130},{6,129},{7,128},{1... | collective-permute-start | bytes 98312 | tf_op jit(solution)/shard_map/ppermute | solution.py:49
  12.1 11.7 %collective-permute-start.6 = (bf16[1,8,16,128]{3,2,1,0:T(8,128)(2,1)}, bf16[1,8,16,128]{3,2,1,0:T(8,128)(2,1)S(1)}, u32[]{:S(2)}, u32[]{:S(2)}) collective-permute-start(bf16[1,8,16,128]{3,2,1,0:T(8,128)(2,1)} %bitcast.23), channel_id=1, source_target_pairs={{0,128},{1,129},{2,130},{3,131},{4,132},{5,133},{6,134},{7,135},{1... | collective-permute-start | bytes 98312 | tf_op jit(solution)/shard_map/ppermute | solution.py:49
  12.5 19.1 %collective-permute-start.3 = (bf16[8,48,128]{2,1,0:T(8,128)(2,1)}, bf16[8,48,128]{2,1,0:T(8,128)(2,1)S(1)}, u32[]{:S(2)}, u32[]{:S(2)}) collective-permute-start(bf16[8,48,128]{2,1,0:T(8,128)(2,1)} %get-tuple-element.42), channel_id=1, source_target_pairs={{0,7},{1,2},{2,1},{3,4},{4,3},{5,6},{6,5},{7,0},{8,15},{9,10},{10,... | collective-permute-start | bytes 294920 | tf_op jit(solution)/shard_map/ppermute | solution.py:49
  13.6 18.1 %collective-permute-start.2 = (bf16[8,48,128]{2,1,0:T(8,128)(2,1)}, bf16[8,48,128]{2,1,0:T(8,128)(2,1)S(1)}, u32[]{:S(2)}, u32[]{:S(2)}) collective-permute-start(bf16[8,48,128]{2,1,0:T(8,128)(2,1)} %get-tuple-element.42), channel_id=1, source_target_pairs={{0,1},{1,0},{2,3},{3,2},{4,5},{5,4},{6,7},{7,6},{8,9},{9,8},{10,11... | collective-permute-start | bytes 294920 | tf_op jit(solution)/shard_map/ppermute | solution.py:49
  13.6 25.2 %collective-permute-start = (bf16[3,768,128]{2,1,0:T(8,128)(2,1)}, bf16[3,768,128]{2,1,0:T(8,128)(2,1)S(1)}, u32[]{:S(2)}, u32[]{:S(2)}) collective-permute-start(bf16[3,768,128]{2,1,0:T(8,128)(2,1)} %get-tuple-element.40), channel_id=1, source_target_pairs={{0,8},{8,0},{16,24},{24,16},{32,40},{40,32},{48,56},{56,48},{64,72... | collective-permute-start | bytes 1769480 | tf_op jit(solution)/shard_map/ppermute | solution.py:49
  14.4 3.8 %copy-start.28 = (f32[5120]{0:T(1024)}, f32[5120]{0:T(1024)S(1)}, u32[]{:S(2)}) copy-start(f32[5120]{0:T(1024)S(1)} %constant_dynamic-update-slice_fusion) | copy-start | bytes 61444
  14.4 3.9 %copy-start.18 = (bf16[3,768,128]{2,1,0:T(8,128)(2,1)S(1)}, bf16[3,768,128]{2,1,0:T(8,128)(2,1)}, u32[]{:S(2)}) copy-start(bf16[3,768,128]{2,1,0:T(8,128)(2,1)} %get-tuple-element.41) | copy-start | bytes 1769476
  18.2 19.2 %copy-start.3 = (bf16[1,8,16,128]{3,2,1,0:T(8,128)(2,1)}, bf16[1,8,16,128]{3,2,1,0:T(8,128)(2,1)S(1)}, u32[]{:S(2)}) copy-start(bf16[1,8,16,128]{3,2,1,0:T(8,128)(2,1)S(1)} %collective-permute-done.7.refs_12_) | copy-start | bytes 98308
  18.3 20.6 %collective-permute-start.1 = (bf16[3,768,128]{2,1,0:T(8,128)(2,1)S(1)}, bf16[3,768,128]{2,1,0:T(8,128)(2,1)S(1)}, u32[]{:S(2)}, u32[]{:S(2)}) collective-permute-start(bf16[3,768,128]{2,1,0:T(8,128)(2,1)S(1)} %copy-done.18), channel_id=1, source_target_pairs={{0,120},{8,16},{16,8},{24,32},{32,24},{40,48},{48,40},{56,64},{64,... | collective-permute-start | bytes 1769480 | tf_op jit(solution)/shard_map/ppermute | solution.py:49
  23.8 13.6 %copy-start.4 = (bf16[1,8,16,128]{3,2,1,0:T(8,128)(2,1)}, bf16[1,8,16,128]{3,2,1,0:T(8,128)(2,1)S(1)}, u32[]{:S(2)}) copy-start(bf16[1,8,16,128]{3,2,1,0:T(8,128)(2,1)S(1)} %collective-permute-done.6.refs_11_) | copy-start | bytes 98308
  23.9 5.9 %collective-permute-start.8 = (bf16[2,8,16,128]{3,2,1,0:T(8,128)(2,1)S(1)}, bf16[2,8,16,128]{3,2,1,0:T(8,128)(2,1)S(1)}, u32[]{:S(2)}, u32[]{:S(2)}) collective-permute-start(bf16[2,8,16,128]{3,2,1,0:T(8,128)(2,1)S(1)} %pad_maximum_fusion.1), channel_id=1, source_target_pairs={{0,2},{1,3},{2,0},{3,1},{4,6},{5,7},{6,4},{7,5},{8,10},{9,11},{10,... | collective-permute-start | bytes 196616 | tf_op jit(solution)/shard_map/ppermute | solution.py:49
  29.8 7.7 %copy-start.5 = (bf16[2,8,16,128]{3,2,1,0:T(8,128)(2,1)}, bf16[2,8,16,128]{3,2,1,0:T(8,128)(2,1)S(1)}, u32[]{:S(2)}) copy-start(bf16[2,8,16,128]{3,2,1,0:T(8,128)(2,1)S(1)} %collective-permute-done.8.refs_13_) | copy-start | bytes 196612
  29.8 9.0 %collective-permute-start.9 = (bf16[4,8,16,128]{3,2,1,0:T(8,128)(2,1)S(1)}, bf16[4,8,16,128]{3,2,1,0:T(8,128)(2,1)S(1)}, u32[]{:S(2)}, u32[]{:S(2)}) collective-permute-start(bf16[4,8,16,128]{3,2,1,0:T(8,128)(2,1)S(1)} %pad_maximum_fusion), channel_id=1, source_target_pairs={{0,1},{1,0},{2,3},{3,2},{4,5},{5,4},{6,7},{7,6},{8,9},{9,8},{10,11... | collective-permute-start | bytes 393224 | tf_op jit(solution)/shard_map/ppermute | solution.py:49
  31.7 5.8 %copy-start.1 = (bf16[8,48,128]{2,1,0:T(8,128)(2,1)}, bf16[8,48,128]{2,1,0:T(8,128)(2,1)S(1)}, u32[]{:S(2)}) copy-start(bf16[8,48,128]{2,1,0:T(8,128)(2,1)S(1)} %broadcast_select_fusion.1.refs_3_) | copy-start | bytes 294916
  31.7 7.1 %collective-permute-start.5 = (bf16[3,48,128]{2,1,0:T(8,128)(2,1)S(1)}, bf16[3,48,128]{2,1,0:T(8,128)(2,1)S(1)}, u32[]{:S(2)}, u32[]{:S(2)}) collective-permute-start(bf16[3,48,128]{2,1,0:T(8,128)(2,1)S(1)} %get-tuple-element.82), channel_id=1, source_target_pairs={{0,120},{8,16},{16,8},{24,32},{32,24},{40,48},{48,40},{56,64},{64,... | collective-permute-start | bytes 110600 | tf_op jit(solution)/shard_map/ppermute | solution.py:49
  31.8 7.0 %collective-permute-start.4 = (bf16[3,48,128]{2,1,0:T(8,128)(2,1)S(1)}, bf16[3,48,128]{2,1,0:T(8,128)(2,1)S(1)}, u32[]{:S(2)}, u32[]{:S(2)}) collective-permute-start(bf16[3,48,128]{2,1,0:T(8,128)(2,1)S(1)} %get-tuple-element.83), channel_id=1, source_target_pairs={{0,8},{8,0},{16,24},{24,16},{32,40},{40,32},{48,56},{56,48},{64,72... | collective-permute-start | bytes 110600 | tf_op jit(solution)/shard_map/ppermute | solution.py:49
  38.8 0.6 copy-start.24
  38.8 0.6 copy-start.26
  38.8 0.7 copy-start.23
  38.8 0.9 copy-start.19
  38.8 1.0 copy-start.20
  71.9 11.2 %collective-permute-start.15 = (bf16[8,48,128]{2,1,0:T(8,128)(2,1)}, bf16[8,48,128]{2,1,0:T(8,128)(2,1)S(1)}, u32[]{:S(2)}, u32[]{:S(2)}) collective-permute-start(bf16[8,48,128]{2,1,0:T(8,128)(2,1)} %get-tuple-element.72), channel_id=1, source_target_pairs={{0,7},{1,2},{2,1},{3,4},{4,3},{5,6},{6,5},{7,0},{8,15},{9,10},{10,... | collective-permute-start | bytes 294920 | tf_op jit(solution)/shard_map/ppermute | solution.py:49
  73.0 10.1 %collective-permute-start.14 = (bf16[8,48,128]{2,1,0:T(8,128)(2,1)}, bf16[8,48,128]{2,1,0:T(8,128)(2,1)S(1)}, u32[]{:S(2)}, u32[]{:S(2)}) collective-permute-start(bf16[8,48,128]{2,1,0:T(8,128)(2,1)} %get-tuple-element.72), channel_id=1, source_target_pairs={{0,1},{1,0},{2,3},{3,2},{4,5},{5,4},{6,7},{7,6},{8,9},{9,8},{10,11... | collective-permute-start | bytes 294920 | tf_op jit(solution)/shard_map/ppermute | solution.py:49
  74.1 9.0 %collective-permute-start.10 = (bf16[4,8,16,128]{3,2,1,0:T(8,128)(2,1)}, bf16[4,8,16,128]{3,2,1,0:T(8,128)(2,1)S(1)}, u32[]{:S(2)}, u32[]{:S(2)}) collective-permute-start(bf16[4,8,16,128]{3,2,1,0:T(8,128)(2,1)} %get-tuple-element.66), channel_id=1, source_target_pairs={{0,1},{1,0},{2,3},{3,2},{4,5},{5,4},{6,7},{7,6},{8,9},{9,8},{10,11... | collective-permute-start | bytes 393224 | tf_op jit(solution)/shard_map/ppermute | solution.py:49
  75.0 17.0 %collective-permute-start.12 = (bf16[3,768,128]{2,1,0:T(8,128)(2,1)}, bf16[3,768,128]{2,1,0:T(8,128)(2,1)S(1)}, u32[]{:S(2)}, u32[]{:S(2)}) collective-permute-start(bf16[3,768,128]{2,1,0:T(8,128)(2,1)} %get-tuple-element.70), channel_id=1, source_target_pairs={{0,8},{8,0},{16,24},{24,16},{32,40},{40,32},{48,56},{56,48},{64,72... | collective-permute-start | bytes 1769480 | tf_op jit(solution)/shard_map/ppermute | solution.py:49
  75.0 17.0 %collective-permute-start.13 = (bf16[3,768,128]{2,1,0:T(8,128)(2,1)}, bf16[3,768,128]{2,1,0:T(8,128)(2,1)S(1)}, u32[]{:S(2)}, u32[]{:S(2)}) collective-permute-start(bf16[3,768,128]{2,1,0:T(8,128)(2,1)} %get-tuple-element.71), channel_id=1, source_target_pairs={{0,120},{8,16},{16,8},{24,32},{32,24},{40,48},{48,40},{56,64},{64,... | collective-permute-start | bytes 1769480 | tf_op jit(solution)/shard_map/ppermute | solution.py:49
  79.2 3.9 %copy-start.2 = (bf16[4,8,16,128]{3,2,1,0:T(8,128)(2,1)S(1)}, bf16[4,8,16,128]{3,2,1,0:T(8,128)(2,1)}, u32[]{:S(2)}) copy-start(bf16[4,8,16,128]{3,2,1,0:T(8,128)(2,1)} %get-tuple-element.65) | copy-start | bytes 393220
  83.1 8.9 %copy-start = (bf16[8,48,128]{2,1,0:T(8,128)(2,1)}, bf16[8,48,128]{2,1,0:T(8,128)(2,1)S(1)}, u32[]{:S(2)}) copy-start(bf16[8,48,128]{2,1,0:T(8,128)(2,1)S(1)} %broadcast_select_fusion.outer_in) | copy-start | bytes 294916
  83.2 5.4 %collective-permute-start.11 = (bf16[2,8,16,128]{3,2,1,0:T(8,128)(2,1)S(1)}, bf16[2,8,16,128]{3,2,1,0:T(8,128)(2,1)S(1)}, u32[]{:S(2)}, u32[]{:S(2)}) collective-permute-start(bf16[2,8,16,128]{3,2,1,0:T(8,128)(2,1)S(1)} %get-tuple-element.77), channel_id=1, source_target_pairs={{0,2},{1,3},{2,0},{3,1},{4,6},{5,7},{6,4},{7,5},{8,10},{9,11},{10,... | collective-permute-start | bytes 196616 | tf_op jit(solution)/shard_map/ppermute | solution.py:49
  84.9 7.1 %collective-permute-start.17 = (bf16[3,48,128]{2,1,0:T(8,128)(2,1)S(1)}, bf16[3,48,128]{2,1,0:T(8,128)(2,1)S(1)}, u32[]{:S(2)}, u32[]{:S(2)}) collective-permute-start(bf16[3,48,128]{2,1,0:T(8,128)(2,1)S(1)} %get-tuple-element.80), channel_id=1, source_target_pairs={{0,120},{8,16},{16,8},{24,32},{32,24},{40,48},{48,40},{56,64},{64,... | collective-permute-start | bytes 110600 | tf_op jit(solution)/shard_map/ppermute | solution.py:49
  85.9 6.1 %collective-permute-start.16 = (bf16[3,48,128]{2,1,0:T(8,128)(2,1)S(1)}, bf16[3,48,128]{2,1,0:T(8,128)(2,1)S(1)}, u32[]{:S(2)}, u32[]{:S(2)}) collective-permute-start(bf16[3,48,128]{2,1,0:T(8,128)(2,1)S(1)} %get-tuple-element.81), channel_id=1, source_target_pairs={{0,8},{8,0},{16,24},{24,16},{32,40},{40,32},{48,56},{56,48},{64,72... | collective-permute-start | bytes 110600 | tf_op jit(solution)/shard_map/ppermute | solution.py:49
  88.5 17.7 %collective-permute-start.19 = (bf16[8,16,128]{2,1,0:T(8,128)(2,1)S(1)}, bf16[8,16,128]{2,1,0:T(8,128)(2,1)S(1)}, u32[]{:S(2)}, u32[]{:S(2)}) collective-permute-start(bf16[8,16,128]{2,1,0:T(8,128)(2,1)S(1)} %get-tuple-element.78), channel_id=1, source_target_pairs={{0,135},{1,134},{2,133},{3,132},{4,131},{5,130},{6,129},{7,128},{1... | collective-permute-start | bytes 98312 | tf_op jit(solution)/shard_map/ppermute | solution.py:49
  92.0 0.6 copy-start.25
  92.0 14.3 %collective-permute-start.18 = (bf16[8,16,128]{2,1,0:T(8,128)(2,1)S(1)}, bf16[8,16,128]{2,1,0:T(8,128)(2,1)S(1)}, u32[]{:S(2)}, u32[]{:S(2)}) collective-permute-start(bf16[8,16,128]{2,1,0:T(8,128)(2,1)S(1)} %get-tuple-element.79), channel_id=1, source_target_pairs={{0,128},{1,129},{2,130},{3,131},{4,132},{5,133},{6,134},{7,135},{1... | collective-permute-start | bytes 98312 | tf_op jit(solution)/shard_map/ppermute | solution.py:49
  92.0 0.6 copy-start.27
  92.0 0.8 copy-start.21
  92.0 1.0 copy-start.22
  106.3 0.6 copy-start.6
  106.3 0.6 copy-start.7

commit v2 on v1

--- a/solution.py
+++ b/solution.py
@@ -768,17 +768,22 @@
     )
 
 
+def east_west(packed, even, odd):
+    first = lax.rem(lax.axis_index("lon"), 2) == 0
+    lane = lax.broadcasted_iota(jnp.int32, packed.shape, 2)
+    return jnp.where((lax.rem(lane, 8) < 4) == first, even, odd)
+
+
+def facing(packed):
+    north = lax.rem(lax.axis_index("lat"), 2) == 1
+    ends = (packed[:3], packed[ROWS - 3 :])
+    return jnp.where(north, ends[0], ends[1]), jnp.where(north, ends[1], ends[0])
+
+
 def swap_outer(packed):
-    first = lax.rem(lax.axis_index("lon"), 2) == 0
-    east_west = [even_swap(packed, "lon"), odd_swap(packed, "lon")]
-    lane = lax.broadcasted_iota(jnp.int32, packed.shape, 2)
-    from_even = (lax.rem(lane, 8) < 4) == first
-    outer = jnp.where(from_even, *east_west)
-    north = lax.rem(lax.axis_index("lat"), 2) == 1
-    ends = (outer[:3], outer[ROWS - 3 :])
-    even = even_swap(jnp.where(north, ends[0], ends[1]), "lat")
-    odd = odd_swap(jnp.where(north, ends[1], ends[0]), "lat")
-    return outer, even, odd
+    outer = east_west(packed, even_swap(packed, "lon"), odd_swap(packed, "lon"))
+    even, odd = facing(outer)
+    return outer, even_swap(even, "lat"), odd_swap(odd, "lat")
 
 
 def cross(block, apart):
@@ -826,8 +831,9 @@
         jnp.tile(ocean_scale, models[1][1]),
         jnp.tile(atmos_scale, models[0][1]),
     )
-    up = scaled_cotangent(cot, wet_mask, scale_rows[:, None])
-    pieces.append(lon_swap(jnp.concatenate(pieces, axis=0), 2))
+    joined, wet_then = lax.optimization_barrier((jnp.concatenate(pieces, axis=0), wet_mask))
+    pieces.append(lon_swap(joined, 2))
+    up = scaled_cotangent(cot, wet_then, scale_rows)
     *pieces, up = lax.optimization_barrier((*pieces, up))
     pieces.append(lon_swap(jnp.concatenate(pieces, axis=0), 1))
     made = ready(
@@ -871,12 +877,16 @@
         weights,
     )
     came = lon_swap(far, 1)
-    around = swap_outer(packed)
+    outer = east_west(packed, even_swap(packed, "lon"), odd_swap(packed, "lon"))
     even = even_swap(even, "lat")
     odd = odd_swap(odd, "lat")
     sums = [(near[k : k + 2].astype(F32) + came[k : k + 2].astype(F32)) for k in (0, 2)]
-    came = lon_swap(sums[1].astype(BF), 2)
-    advanced = advance(advanced, wet_mask)
+    lot, *corners, wet_then = lax.optimization_barrier(
+        (sums[1].astype(BF), *facing(outer), wet_mask)
+    )
+    came = lon_swap(lot, 2)
+    around = (outer, even_swap(corners[0], "lat"), odd_swap(corners[1], "lat"))
+    advanced = advance(advanced, wet_then)
     came, advanced = lax.optimization_barrier((came, advanced))
     ends = [(sums[0][k] + came[k].astype(F32)).astype(BF) for k in range(2)]
     coupling = cross(ends[0], 0), cross(ends[1], 7)

time: 111 us -> 109 us (0.982); the launches traced: 109 us -> 108 us
  waiting for transfers between devices: 10.7 us -> 1.7 us
  starting transfers between devices: 28.7 us -> 36.6 us
    ppermute x20, waiting for transfers between devices: 10.7 us -> 1.7 us  [swap(): return lax.ppermute(block, axes, route)]
    ppermute x20, starting transfers between devices: 28.7 us -> 36.6 us  [swap(): return lax.ppermute(block, axes, route)]
    unnamed x67 -> x63, local copies, waits for them, and re-layouts: 2.77 us -> 2.77 us
  transfers between devices with their start and end apart: 20 -> 20, of which waited for: 4 -> 2; matrix products, arithmetic and copies ran while one was open for 1% -> 2% of each run, Pallas kernels for 24% -> 24%
where the time goes in v2:
time: 109 us; the launch traced here: 108 us
  Pallas kernels  64.4 us (59%)
  starting transfers between devices  36.6 us (34%)
  local copies, waits for them, and re-layouts  2.79 us (3%)
  waiting for transfers between devices  1.7 us (2%)
  other arithmetic  1.61 us (1%)
  between operations  1.34 us (1%)
    ppermute x20, starting transfers between devices, swap(): return lax.ppermute(block, axes, route)  36.6 us
    pallas_call x1, Pallas kernels, cells(): pl.pallas_call(functools.partial(cells_kernel, models), in_specs=[ANY] *...  32 us
    pallas_call x1, Pallas kernels, adjoint(): pl.pallas_call(functools.partial(adjoint_kernel, models), in_specs=[ANY]...  13.2 us
    pallas_call x1, Pallas kernels, ready(): pl.pallas_call(functools.partial(ready_kernel, models), in_specs=[VMEM] *...  5.56 us
    pallas_call x1, Pallas kernels, prepare(): pl.pallas_call(prepare_kernel, grid=(stacked // part,), in_specs=[pl.Bloc...  4.41 us
    pallas_call x1, Pallas kernels, advance(): pl.pallas_call(advance_kernel, grid=(stacked // part,), in_specs=[pl.Bloc...  3.83 us
    pallas_call x1, Pallas kernels, scaled_cotangent(): pl.pallas_call(cotangent_kernel, grid=(stacked // part,), in_specs=[pl.Bl...  3.77 us
    unnamed x63, local copies, waits for them, and re-layouts  2.77 us
  transfers between devices with their start and end apart: 20, of which 2 were waited for; matrix products, arithmetic and copies ran while one was open for 2% of the time, Pallas kernels for 24%

profile of v2, /device:TPU:32, one launch (start us, length us, event | category | flops | bytes accessed | tf_op | source)
XLA Modules:
  0.0 108.4 jit_solution(16458194342502620948)
XLA Ops:
  0.7 4.4 %prepare.1 = (bf16[8,768,128]{2,1,0:T(8,128)(2,1)}, bf16[3,768,128]{2,1,0:T(8,128)(2,1)}, bf16[3,768,128]{2,1,0:T(8,128)(2,1)}, bf16[8,16,128]{2,1,0:T(8,128)(2,1)}, bf16[8,48,128]{2,1,0:T(8,128)(2,1)}) custom-call(bf16[768,8,128]{2,1,0:T(8,128)(2,1)} %bitcast.14, s32[8,128]{1,0:T(8,128)} %wet_ref.7), custom_call_target="tpu_custom_call" | custom-call | flops 1000000 | bytes 5000000 | tf_op jit(solution)/shard_map/prepare/pallas_call | solution.py:111
  5.2 6.9 %collective-permute-start.7 = (bf16[1,8,16,128]{3,2,1,0:T(8,128)(2,1)}, bf16[1,8,16,128]{3,2,1,0:T(8,128)(2,1)S(1)}, u32[]{:S(2)}, u32[]{:S(2)}) collective-permute-start(bf16[1,8,16,128]{3,2,1,0:T(8,128)(2,1)} %bitcast.22), channel_id=1, source_target_pairs={{0,135},{1,134},{2,133},{3,132},{4,131},{5,130},{6,129},{7,128},{1... | collective-permute-start | bytes 98312 | tf_op jit(solution)/shard_map/ppermute | solution.py:49
  12.1 0.5 collective-permute-start.6
  12.5 1.0 collective-permute-start.3
  13.6 0.0 collective-permute-start.2
  13.6 0.0 collective-permute-start
  13.6 0.0 copy-done.8
  13.7 0.0 copy-done.14
  13.8 0.0 copy-done.16
  13.8 0.6 broadcast_select_fusion.6.scale_ref
  14.4 0.0 collective-permute-done.7.refs_12_
  14.4 5.6 %collective-permute-start.1 = (bf16[3,768,128]{2,1,0:T(8,128)(2,1)}, bf16[3,768,128]{2,1,0:T(8,128)(2,1)S(1)}, u32[]{:S(2)}, u32[]{:S(2)}) collective-permute-start(bf16[3,768,128]{2,1,0:T(8,128)(2,1)} %get-tuple-element.47), channel_id=1, source_target_pairs={{0,120},{8,16},{16,8},{24,32},{32,24},{40,48},{48,40},{56,64},{64,... | collective-permute-start | bytes 1769480 | tf_op jit(solution)/shard_map/ppermute | solution.py:49
  20.0 0.0 collective-permute-done.6.refs_11_
  20.0 2.6 %collective-permute-start.8 = (bf16[2,8,16,128]{3,2,1,0:T(8,128)(2,1)S(1)}, bf16[2,8,16,128]{3,2,1,0:T(8,128)(2,1)S(1)}, u32[]{:S(2)}, u32[]{:S(2)}) collective-permute-start(bf16[2,8,16,128]{3,2,1,0:T(8,128)(2,1)S(1)} %pad_maximum_fusion.1), channel_id=1, source_target_pairs={{0,2},{1,3},{2,0},{3,1},{4,6},{5,7},{6,4},{7,5},{8,10},{9,11},{10,... | collective-permute-start | bytes 196616 | tf_op jit(solution)/shard_map/ppermute | solution.py:49
  22.6 3.8 %scaled_cotangent.1.refs_7_ = bf16[8,768,128]{2,1,0:T(8,128)(2,1)} custom-call(bf16[768,8,128]{2,1,0:T(8,128)(2,1)} %bitcast.15, s32[8,128]{1,0:T(8,128)} %wet_ref.7, f32[3,1,256]{2,1,0:T(1,128)} %broadcast_select_fusion.6.scale_ref), custom_call_target="tpu_custom_call" | custom-call | flops 1000000 | bytes 4000000 | tf_op jit(solution)/shard_map/scaled_cotangent/pallas_call | solution.py:217
  26.4 0.0 collective-permute-done.8.refs_13_
  26.4 1.1 %collective-permute-start.9 = (bf16[4,8,16,128]{3,2,1,0:T(8,128)(2,1)S(1)}, bf16[4,8,16,128]{3,2,1,0:T(8,128)(2,1)S(1)}, u32[]{:S(2)}, u32[]{:S(2)}) collective-permute-start(bf16[4,8,16,128]{3,2,1,0:T(8,128)(2,1)S(1)} %pad_maximum_fusion), channel_id=1, source_target_pairs={{0,1},{1,0},{2,3},{3,2},{4,5},{5,4},{6,7},{7,6},{8,9},{9,8},{10,11... | collective-permute-start | bytes 393224 | tf_op jit(solution)/shard_map/ppermute | solution.py:49
  27.5 0.0 collective-permute-done.3
  27.6 0.0 collective-permute-done.2
  27.6 0.1 collective-permute-start.5
  27.7 0.1 collective-permute-start.4
  27.8 5.6 %ready.1 = (bf16[1536,384]{1,0:T(8,128)(2,1)}, bf16[384,1536]{1,0:T(8,128)(2,1)}, f32[1536,128]{1,0:T(8,128)}, f32[4,384,128]{2,1,0:T(8,128)}, bf16[2,7,384,128]{3,2,1,0:T(8,128)(2,1)}) custom-call(f32[1,5120]{1,0:T(1,128)} %bitcast.24, bf16[384,1536]{1,0:T(8,128)(2,1)} %refs_15_.1, bf16[1536,384]{1,0:T(8,128)(2,1)} %refs_16_.1, f32[49,384]{1,0:T(8,128)} %bitcast.20, ...), custom_call_target="tpu_custom_call" | custom-call | flops 1000000000 | bytes 10000000 | tf_op jit(solution)/shard_map/ready/pallas_call | solution.py:181
  33.4 0.0 copy-done.1
  33.4 1.3 %collective-permute-done.5.refs_5_ = bf16[3,48,128]{2,1,0:T(8,128)(2,1)S(1)} collective-permute-done((bf16[3,48,128]{2,1,0:T(8,128)(2,1)S(1)}, bf16[3,48,128]{2,1,0:T(8,128)(2,1)S(1)}, u32[]{:S(2)}, u32[]{:S(2)}) %collective-permute-start.5) | collective-permute-done | bytes 36896 | tf_op jit(solution)/shard_map/ppermute | solution.py:49
  34.7 0.0 collective-permute-done.4.refs_4_
  34.7 0.0 collective-permute-done.9.refs_14_
  34.7 0.0 collective-permute-done.refs_1_
  34.7 0.0 copy-start.17
  34.7 0.0 collective-permute-done.1.refs_2_
  34.8 0.5 copy-done.22
  35.3 0.0 copy-done.24
  35.3 0.1 copy-done.21
  35.4 0.2 copy-done.17
  35.6 0.2 copy-done.18
  35.8 32.0 %cells.1 = (bf16[8,768,128]{2,1,0:T(8,128)(2,1)}, bf16[8,768,128]{2,1,0:T(8,128)(2,1)}, bf16[3,768,128]{2,1,0:T(8,128)(2,1)}, bf16[3,768,128]{2,1,0:T(8,128)(2,1...) custom-call(bf16[8,768,128]{2,1,0:T(8,128)(2,1)} %get-tuple-element.45.refs_0_, ...), custom_call_target="tpu_custom_call" | custom-call | flops 10000000000 | bytes 20000000 | tf_op jit(solution)/shard_map/cells/pallas_call | solution.py:705
  67.8 1.1 %collective-permute-start.12 = (bf16[8,48,128]{2,1,0:T(8,128)(2,1)}, bf16[8,48,128]{2,1,0:T(8,128)(2,1)S(1)}, u32[]{:S(2)}, u32[]{:S(2)}) collective-permute-start(bf16[8,48,128]{2,1,0:T(8,128)(2,1)} %get-tuple-element.75), channel_id=1, source_target_pairs={{0,7},{1,2},{2,1},{3,4},{4,3},{5,6},{6,5},{7,0},{8,15},{9,10},{10,... | collective-permute-start | bytes 294920 | tf_op jit(solution)/shard_map/ppermute | solution.py:49
  68.9 1.4 %collective-permute-start.11 = (bf16[8,48,128]{2,1,0:T(8,128)(2,1)}, bf16[8,48,128]{2,1,0:T(8,128)(2,1)S(1)}, u32[]{:S(2)}, u32[]{:S(2)}) collective-permute-start(bf16[8,48,128]{2,1,0:T(8,128)(2,1)} %get-tuple-element.75), channel_id=1, source_target_pairs={{0,1},{1,0},{2,3},{3,2},{4,5},{5,4},{6,7},{7,6},{8,9},{9,8},{10,11... | collective-permute-start | bytes 294920 | tf_op jit(solution)/shard_map/ppermute | solution.py:49
  70.3 0.6 collective-permute-start.10
  70.9 0.0 collective-permute-start.14
  70.9 4.2 %collective-permute-start.15 = (bf16[3,768,128]{2,1,0:T(8,128)(2,1)}, bf16[3,768,128]{2,1,0:T(8,128)(2,1)S(1)}, u32[]{:S(2)}, u32[]{:S(2)}) collective-permute-start(bf16[3,768,128]{2,1,0:T(8,128)(2,1)} %get-tuple-element.82), channel_id=1, source_target_pairs={{0,120},{8,16},{16,8},{24,32},{32,24},{40,48},{48,40},{56,64},{64,... | collective-permute-start | bytes 1769480 | tf_op jit(solution)/shard_map/ppermute | solution.py:49
  75.1 0.0 collective-permute-done.12
  75.1 0.0 collective-permute-done.11
  75.2 0.3 collective-permute-done.10
  75.5 0.9 convert_add_fusion
  76.4 1.7 %collective-permute-start.13 = (bf16[2,8,16,128]{3,2,1,0:T(8,128)(2,1)S(1)}, bf16[2,8,16,128]{3,2,1,0:T(8,128)(2,1)S(1)}, u32[]{:S(2)}, u32[]{:S(2)}) collective-permute-start(bf16[2,8,16,128]{3,2,1,0:T(8,128)(2,1)S(1)} %get-tuple-element.76), channel_id=1, source_target_pairs={{0,2},{1,3},{2,0},{3,1},{4,6},{5,7},{6,4},{7,5},{8,10},{9,11},{10,... | collective-permute-start | bytes 196616 | tf_op jit(solution)/shard_map/ppermute | solution.py:49
  78.1 0.0 collective-permute-start.16
  78.1 5.5 %collective-permute-start.17 = (bf16[3,48,128]{2,1,0:T(8,128)(2,1)S(1)}, bf16[3,48,128]{2,1,0:T(8,128)(2,1)S(1)}, u32[]{:S(2)}, u32[]{:S(2)}) collective-permute-start(bf16[3,48,128]{2,1,0:T(8,128)(2,1)S(1)} %get-tuple-element.84), channel_id=1, source_target_pairs={{0,120},{8,16},{16,8},{24,32},{32,24},{40,48},{48,40},{56,64},{64,... | collective-permute-start | bytes 110600 | tf_op jit(solution)/shard_map/ppermute | solution.py:49
  83.6 3.8 %advance.1 = bf16[768,8,128]{2,1,0:T(8,128)(2,1)} custom-call(bf16[8,768,128]{2,1,0:T(8,128)(2,1)} %get-tuple-element.77.rows_ref, s32[8,128]{1,0:T(8,128)} %wet_ref.7), custom_call_target="tpu_custom_call" | custom-call | flops 1000000 | bytes 4000000 | tf_op jit(solution)/shard_map/advance/pallas_call | solution.py:461
  87.5 0.0 collective-permute-done.13
  87.5 0.1 collective-permute-start.19
  87.6 0.0 collective-permute-done.16.corner_even
  87.6 4.1 %collective-permute-start.18 = (bf16[8,16,128]{2,1,0:T(8,128)(2,1)S(1)}, bf16[8,16,128]{2,1,0:T(8,128)(2,1)S(1)}, u32[]{:S(2)}, u32[]{:S(2)}) collective-permute-start(bf16[8,16,128]{2,1,0:T(8,128)(2,1)S(1)} %get-tuple-element.91), channel_id=1, source_target_pairs={{0,128},{1,129},{2,130},{3,131},{4,132},{5,133},{6,134},{7,135},{1... | collective-permute-start | bytes 98312 | tf_op jit(solution)/shard_map/ppermute | solution.py:49
  91.7 0.0 collective-permute-done.17.corner_odd
  91.8 0.0 collective-permute-done.14.even_hbm
  91.8 0.0 collective-permute-done.15.odd_hbm
  91.8 0.6 copy-done.25
  92.4 0.2 copy-done.19
  92.6 0.2 copy-done.20
  92.8 13.2 %adjoint.1 = (f32[2,16,8,128]{3,2,1,0:T(8,128)}, bf16[768,8,128]{2,1,0:T(8,128)(2,1)}) custom-call(bf16[8,768,128]{2,1,0:T(8,128)(2,1)} %get-tuple-element.80.rows_hbm, bf16[3,768,128]{2,1,0:T(8,128)(2,1)} %copy-done.19, bf16[3,768,128]{2,1,0:T(8,128)(2,1)} %copy-done.20, bf16[8,48,128]{2,1,0:T(8,128)(2,1)} %copy-done, bf16[3,48,128]{2,1,0:T(8,128)(2,1)} %copy-done.23, ...), custom_call_target="tpu_custom_call" | custom-call | flops 3000000000 | bytes 8000000 | tf_op jit(solution)/shard_map/adjoint/pallas_call | solution.py:402
  106.0 0.0 collective-permute-done.19.far_ref
  106.0 0.0 collective-permute-done.18.near_ref
  106.0 0.6 copy-done.5
  106.6 0.0 copy-done.6
  106.6 1.6 %couple.1 = bf16[768,8,128]{2,1,0:T(8,128)(2,1)} custom-call(f32[2,16,8,128]{3,2,1,0:T(8,128)} %get-tuple-element.85.first_ref, bf16[8,16,128]{2,1,0:T(8,128)(2,1)} %copy-done.6, bf16[8,16,128]{2,1,0:T(8,128)(2,1)} %copy-done.5, s32[8,128]{1,0:T(8,128)} %wet_ref.7, bf16[768,8,128]{2,1,0:T(8,128)(2,1)} %get-tuple-element.87._), custom_call_target="tpu_custom_call", output_to_operand_aliasing={{}: (4, {})} | custom-call | flops 100000 | bytes 1000000 | tf_op jit(solution)/shard_map/couple/pallas_call | solution.py:433
  (60 shorter events, 0.3 us)
Async XLA Ops:
  0.6 12.9 %copy-start.8 = (f32[384]{0:T(512)S(1)}, f32[384]{0:T(512)}, u32[]{:S(2)}) copy-start(f32[384]{0:T(512)} %param.31) | copy-start | bytes 4612
  0.6 13.0 %copy-start.7 = (f32[1536]{0:T(1024)S(1)}, f32[1536]{0:T(1024)}, u32[]{:S(2)}) copy-start(f32[1536]{0:T(1024)} %param.28) | copy-start | bytes 18436
  0.7 13.0 %copy-start.11 = (f32[384]{0:T(512)S(1)}, f32[384]{0:T(512)}, u32[]{:S(2)}) copy-start(f32[384]{0:T(512)} %param.25) | copy-start | bytes 4612
  0.7 13.0 %copy-start.12 = (f32[384]{0:T(512)S(1)}, f32[384]{0:T(512)}, u32[]{:S(2)}) copy-start(f32[384]{0:T(512)} %param.26) | copy-start | bytes 4612
  0.7 13.0 %copy-start.13 = (f32[384]{0:T(512)S(1)}, f32[384]{0:T(512)}, u32[]{:S(2)}) copy-start(f32[384]{0:T(512)} %param.30) | copy-start | bytes 4612
  0.7 13.0 %copy-start.10 = (f32[1024]{0:T(1024)S(1)}, f32[1024]{0:T(1024)}, u32[]{:S(2)}) copy-start(f32[1024]{0:T(1024)} %param.36) | copy-start | bytes 12292
  0.7 13.0 %copy-start.14 = (f32[256]{0:T(256)S(1)}, f32[256]{0:T(256)}, u32[]{:S(2)}) copy-start(f32[256]{0:T(256)} %param.33) | copy-start | bytes 3076
  0.7 13.0 %copy-start.15 = (f32[256]{0:T(256)S(1)}, f32[256]{0:T(256)}, u32[]{:S(2)}) copy-start(f32[256]{0:T(256)} %param.34) | copy-start | bytes 3076
  0.7 13.1 %copy-start.16 = (f32[256]{0:T(256)S(1)}, f32[256]{0:T(256)}, u32[]{:S(2)}) copy-start(f32[256]{0:T(256)} %param.38) | copy-start | bytes 3076
  0.7 13.1 %copy-start.9 = (f32[256]{0:T(256)S(1)}, f32[256]{0:T(256)}, u32[]{:S(2)}) copy-start(f32[256]{0:T(256)} %param.39) | copy-start | bytes 3076
  5.2 9.3 %collective-permute-start.7 = (bf16[1,8,16,128]{3,2,1,0:T(8,128)(2,1)}, bf16[1,8,16,128]{3,2,1,0:T(8,128)(2,1)S(1)}, u32[]{:S(2)}, u32[]{:S(2)}) collective-permute-start(bf16[1,8,16,128]{3,2,1,0:T(8,128)(2,1)} %bitcast.22), channel_id=1, source_target_pairs={{0,135},{1,134},{2,133},{3,132},{4,131},{5,130},{6,129},{7,128},{1... | collective-permute-start | bytes 98312 | tf_op jit(solution)/shard_map/ppermute | solution.py:49
  12.1 7.9 %collective-permute-start.6 = (bf16[1,8,16,128]{3,2,1,0:T(8,128)(2,1)}, bf16[1,8,16,128]{3,2,1,0:T(8,128)(2,1)S(1)}, u32[]{:S(2)}, u32[]{:S(2)}) collective-permute-start(bf16[1,8,16,128]{3,2,1,0:T(8,128)(2,1)} %bitcast.23), channel_id=1, source_target_pairs={{0,128},{1,129},{2,130},{3,131},{4,132},{5,133},{6,134},{7,135},{1... | collective-permute-start | bytes 98312 | tf_op jit(solution)/shard_map/ppermute | solution.py:49
  12.5 15.0 %collective-permute-start.3 = (bf16[8,48,128]{2,1,0:T(8,128)(2,1)}, bf16[8,48,128]{2,1,0:T(8,128)(2,1)S(1)}, u32[]{:S(2)}, u32[]{:S(2)}) collective-permute-start(bf16[8,48,128]{2,1,0:T(8,128)(2,1)} %get-tuple-element.48), channel_id=1, source_target_pairs={{0,7},{1,2},{2,1},{3,4},{4,3},{5,6},{6,5},{7,0},{8,15},{9,10},{10,... | collective-permute-start | bytes 294920 | tf_op jit(solution)/shard_map/ppermute | solution.py:49
  13.6 14.0 %collective-permute-start.2 = (bf16[8,48,128]{2,1,0:T(8,128)(2,1)}, bf16[8,48,128]{2,1,0:T(8,128)(2,1)S(1)}, u32[]{:S(2)}, u32[]{:S(2)}) collective-permute-start(bf16[8,48,128]{2,1,0:T(8,128)(2,1)} %get-tuple-element.48), channel_id=1, source_target_pairs={{0,1},{1,0},{2,3},{3,2},{4,5},{5,4},{6,7},{7,6},{8,9},{9,8},{10,11... | collective-permute-start | bytes 294920 | tf_op jit(solution)/shard_map/ppermute | solution.py:49
  13.6 21.2 %collective-permute-start = (bf16[3,768,128]{2,1,0:T(8,128)(2,1)}, bf16[3,768,128]{2,1,0:T(8,128)(2,1)S(1)}, u32[]{:S(2)}, u32[]{:S(2)}) collective-permute-start(bf16[3,768,128]{2,1,0:T(8,128)(2,1)} %get-tuple-element.46), channel_id=1, source_target_pairs={{0,8},{8,0},{16,24},{24,16},{32,40},{40,32},{48,56},{56,48},{64,72... | collective-permute-start | bytes 1769480 | tf_op jit(solution)/shard_map/ppermute | solution.py:49
  14.4 11.9 %copy-start.26 = (f32[5120]{0:T(1024)}, f32[5120]{0:T(1024)S(1)}, u32[]{:S(2)}) copy-start(f32[5120]{0:T(1024)S(1)} %constant_dynamic-update-slice_fusion) | copy-start | bytes 61444
  14.4 11.9 %copy-start.2 = (bf16[1,8,16,128]{3,2,1,0:T(8,128)(2,1)}, bf16[1,8,16,128]{3,2,1,0:T(8,128)(2,1)S(1)}, u32[]{:S(2)}) copy-start(bf16[1,8,16,128]{3,2,1,0:T(8,128)(2,1)S(1)} %collective-permute-done.7.refs_12_) | copy-start | bytes 98308
  14.4 20.3 %collective-permute-start.1 = (bf16[3,768,128]{2,1,0:T(8,128)(2,1)}, bf16[3,768,128]{2,1,0:T(8,128)(2,1)S(1)}, u32[]{:S(2)}, u32[]{:S(2)}) collective-permute-start(bf16[3,768,128]{2,1,0:T(8,128)(2,1)} %get-tuple-element.47), channel_id=1, source_target_pairs={{0,120},{8,16},{16,8},{24,32},{32,24},{40,48},{48,40},{56,64},{64,... | collective-permute-start | bytes 1769480 | tf_op jit(solution)/shard_map/ppermute | solution.py:49
  20.0 6.4 %copy-start.3 = (bf16[1,8,16,128]{3,2,1,0:T(8,128)(2,1)}, bf16[1,8,16,128]{3,2,1,0:T(8,128)(2,1)S(1)}, u32[]{:S(2)}) copy-start(bf16[1,8,16,128]{3,2,1,0:T(8,128)(2,1)S(1)} %collective-permute-done.6.refs_11_) | copy-start | bytes 98308
  20.0 6.3 %collective-permute-start.8 = (bf16[2,8,16,128]{3,2,1,0:T(8,128)(2,1)S(1)}, bf16[2,8,16,128]{3,2,1,0:T(8,128)(2,1)S(1)}, u32[]{:S(2)}, u32[]{:S(2)}) collective-permute-start(bf16[2,8,16,128]{3,2,1,0:T(8,128)(2,1)S(1)} %pad_maximum_fusion.1), channel_id=1, source_target_pairs={{0,2},{1,3},{2,0},{3,1},{4,6},{5,7},{6,4},{7,5},{8,10},{9,11},{10,... | collective-permute-start | bytes 196616 | tf_op jit(solution)/shard_map/ppermute | solution.py:49
  26.4 7.0 %copy-start.4 = (bf16[2,8,16,128]{3,2,1,0:T(8,128)(2,1)}, bf16[2,8,16,128]{3,2,1,0:T(8,128)(2,1)S(1)}, u32[]{:S(2)}) copy-start(bf16[2,8,16,128]{3,2,1,0:T(8,128)(2,1)S(1)} %collective-permute-done.8.refs_13_) | copy-start | bytes 196612
  26.4 8.3 %collective-permute-start.9 = (bf16[4,8,16,128]{3,2,1,0:T(8,128)(2,1)S(1)}, bf16[4,8,16,128]{3,2,1,0:T(8,128)(2,1)S(1)}, u32[]{:S(2)}, u32[]{:S(2)}) collective-permute-start(bf16[4,8,16,128]{3,2,1,0:T(8,128)(2,1)S(1)} %pad_maximum_fusion), channel_id=1, source_target_pairs={{0,1},{1,0},{2,3},{3,2},{4,5},{5,4},{6,7},{7,6},{8,9},{9,8},{10,11... | collective-permute-start | bytes 393224 | tf_op jit(solution)/shard_map/ppermute | solution.py:49
  27.6 5.8 %copy-start.1 = (bf16[8,48,128]{2,1,0:T(8,128)(2,1)}, bf16[8,48,128]{2,1,0:T(8,128)(2,1)S(1)}, u32[]{:S(2)}) copy-start(bf16[8,48,128]{2,1,0:T(8,128)(2,1)S(1)} %broadcast_select_fusion.1.refs_3_) | copy-start | bytes 294916
  27.6 7.1 %collective-permute-start.5 = (bf16[3,48,128]{2,1,0:T(8,128)(2,1)S(1)}, bf16[3,48,128]{2,1,0:T(8,128)(2,1)S(1)}, u32[]{:S(2)}, u32[]{:S(2)}) collective-permute-start(bf16[3,48,128]{2,1,0:T(8,128)(2,1)S(1)} %get-tuple-element.94), channel_id=1, source_target_pairs={{0,120},{8,16},{16,8},{24,32},{32,24},{40,48},{48,40},{56,64},{64,... | collective-permute-start | bytes 110600 | tf_op jit(solution)/shard_map/ppermute | solution.py:49
  27.7 7.0 %collective-permute-start.4 = (bf16[3,48,128]{2,1,0:T(8,128)(2,1)S(1)}, bf16[3,48,128]{2,1,0:T(8,128)(2,1)S(1)}, u32[]{:S(2)}, u32[]{:S(2)}) collective-permute-start(bf16[3,48,128]{2,1,0:T(8,128)(2,1)S(1)} %get-tuple-element.95), channel_id=1, source_target_pairs={{0,8},{8,0},{16,24},{24,16},{32,40},{40,32},{48,56},{56,48},{64,72... | collective-permute-start | bytes 110600 | tf_op jit(solution)/shard_map/ppermute | solution.py:49
  34.7 0.6 copy-start.22
  34.7 0.6 copy-start.24
  34.7 0.7 copy-start.21
  34.7 0.9 copy-start.17
  34.7 1.1 copy-start.18
  67.8 7.3 %collective-permute-start.12 = (bf16[8,48,128]{2,1,0:T(8,128)(2,1)}, bf16[8,48,128]{2,1,0:T(8,128)(2,1)S(1)}, u32[]{:S(2)}, u32[]{:S(2)}) collective-permute-start(bf16[8,48,128]{2,1,0:T(8,128)(2,1)} %get-tuple-element.75), channel_id=1, source_target_pairs={{0,7},{1,2},{2,1},{3,4},{4,3},{5,6},{6,5},{7,0},{8,15},{9,10},{10,... | collective-permute-start | bytes 294920 | tf_op jit(solution)/shard_map/ppermute | solution.py:49
  68.9 6.2 %collective-permute-start.11 = (bf16[8,48,128]{2,1,0:T(8,128)(2,1)}, bf16[8,48,128]{2,1,0:T(8,128)(2,1)S(1)}, u32[]{:S(2)}, u32[]{:S(2)}) collective-permute-start(bf16[8,48,128]{2,1,0:T(8,128)(2,1)} %get-tuple-element.75), channel_id=1, source_target_pairs={{0,1},{1,0},{2,3},{3,2},{4,5},{5,4},{6,7},{7,6},{8,9},{9,8},{10,11... | collective-permute-start | bytes 294920 | tf_op jit(solution)/shard_map/ppermute | solution.py:49
  70.3 5.2 %collective-permute-start.10 = (bf16[4,8,16,128]{3,2,1,0:T(8,128)(2,1)}, bf16[4,8,16,128]{3,2,1,0:T(8,128)(2,1)S(1)}, u32[]{:S(2)}, u32[]{:S(2)}) collective-permute-start(bf16[4,8,16,128]{3,2,1,0:T(8,128)(2,1)} %get-tuple-element.74), channel_id=1, source_target_pairs={{0,1},{1,0},{2,3},{3,2},{4,5},{5,4},{6,7},{7,6},{8,9},{9,8},{10,11... | collective-permute-start | bytes 393224 | tf_op jit(solution)/shard_map/ppermute | solution.py:49
  70.9 20.8 %collective-permute-start.14 = (bf16[3,768,128]{2,1,0:T(8,128)(2,1)}, bf16[3,768,128]{2,1,0:T(8,128)(2,1)S(1)}, u32[]{:S(2)}, u32[]{:S(2)}) collective-permute-start(bf16[3,768,128]{2,1,0:T(8,128)(2,1)} %get-tuple-element.81), channel_id=1, source_target_pairs={{0,8},{8,0},{16,24},{24,16},{32,40},{40,32},{48,56},{56,48},{64,72... | collective-permute-start | bytes 1769480 | tf_op jit(solution)/shard_map/ppermute | solution.py:49
  70.9 20.8 %collective-permute-start.15 = (bf16[3,768,128]{2,1,0:T(8,128)(2,1)}, bf16[3,768,128]{2,1,0:T(8,128)(2,1)S(1)}, u32[]{:S(2)}, u32[]{:S(2)}) collective-permute-start(bf16[3,768,128]{2,1,0:T(8,128)(2,1)} %get-tuple-element.82), channel_id=1, source_target_pairs={{0,120},{8,16},{16,8},{24,32},{32,24},{40,48},{48,40},{56,64},{64,... | collective-permute-start | bytes 1769480 | tf_op jit(solution)/shard_map/ppermute | solution.py:49
  75.1 12.3 %copy-start = (bf16[8,48,128]{2,1,0:T(8,128)(2,1)}, bf16[8,48,128]{2,1,0:T(8,128)(2,1)S(1)}, u32[]{:S(2)}) copy-start(bf16[8,48,128]{2,1,0:T(8,128)(2,1)S(1)} %broadcast_select_fusion.outer_in) | copy-start | bytes 294916
  76.4 11.0 %collective-permute-start.13 = (bf16[2,8,16,128]{3,2,1,0:T(8,128)(2,1)S(1)}, bf16[2,8,16,128]{3,2,1,0:T(8,128)(2,1)S(1)}, u32[]{:S(2)}, u32[]{:S(2)}) collective-permute-start(bf16[2,8,16,128]{3,2,1,0:T(8,128)(2,1)S(1)} %get-tuple-element.76), channel_id=1, source_target_pairs={{0,2},{1,3},{2,0},{3,1},{4,6},{5,7},{6,4},{7,5},{8,10},{9,11},{10,... | collective-permute-start | bytes 196616 | tf_op jit(solution)/shard_map/ppermute | solution.py:49
  78.1 9.5 %collective-permute-start.16 = (bf16[3,48,128]{2,1,0:T(8,128)(2,1)S(1)}, bf16[3,48,128]{2,1,0:T(8,128)(2,1)S(1)}, u32[]{:S(2)}, u32[]{:S(2)}) collective-permute-start(bf16[3,48,128]{2,1,0:T(8,128)(2,1)S(1)} %get-tuple-element.83), channel_id=1, source_target_pairs={{0,8},{8,0},{16,24},{24,16},{32,40},{40,32},{48,56},{56,48},{64,72... | collective-permute-start | bytes 110600 | tf_op jit(solution)/shard_map/ppermute | solution.py:49
  78.1 13.6 %collective-permute-start.17 = (bf16[3,48,128]{2,1,0:T(8,128)(2,1)S(1)}, bf16[3,48,128]{2,1,0:T(8,128)(2,1)S(1)}, u32[]{:S(2)}, u32[]{:S(2)}) collective-permute-start(bf16[3,48,128]{2,1,0:T(8,128)(2,1)S(1)} %get-tuple-element.84), channel_id=1, source_target_pairs={{0,120},{8,16},{16,8},{24,32},{32,24},{40,48},{48,40},{56,64},{64,... | collective-permute-start | bytes 110600 | tf_op jit(solution)/shard_map/ppermute | solution.py:49
  87.5 18.5 %collective-permute-start.19 = (bf16[8,16,128]{2,1,0:T(8,128)(2,1)S(1)}, bf16[8,16,128]{2,1,0:T(8,128)(2,1)S(1)}, u32[]{:S(2)}, u32[]{:S(2)}) collective-permute-start(bf16[8,16,128]{2,1,0:T(8,128)(2,1)S(1)} %get-tuple-element.90), channel_id=1, source_target_pairs={{0,135},{1,134},{2,133},{3,132},{4,131},{5,130},{6,129},{7,128},{1... | collective-permute-start | bytes 98312 | tf_op jit(solution)/shard_map/ppermute | solution.py:49
  87.6 4.2 %copy-start.23 = (bf16[3,48,128]{2,1,0:T(8,128)(2,1)}, bf16[3,48,128]{2,1,0:T(8,128)(2,1)S(1)}, u32[]{:S(2)}) copy-start(bf16[3,48,128]{2,1,0:T(8,128)(2,1)S(1)} %collective-permute-done.16.corner_even) | copy-start | bytes 110596
  87.6 18.4 %collective-permute-start.18 = (bf16[8,16,128]{2,1,0:T(8,128)(2,1)S(1)}, bf16[8,16,128]{2,1,0:T(8,128)(2,1)S(1)}, u32[]{:S(2)}, u32[]{:S(2)}) collective-permute-start(bf16[8,16,128]{2,1,0:T(8,128)(2,1)S(1)} %get-tuple-element.91), channel_id=1, source_target_pairs={{0,128},{1,129},{2,130},{3,131},{4,132},{5,133},{6,134},{7,135},{1... | collective-permute-start | bytes 98312 | tf_op jit(solution)/shard_map/ppermute | solution.py:49
  91.8 0.6 copy-start.25
  91.8 0.8 copy-start.19
  91.8 1.0 copy-start.20
  106.0 0.6 copy-start.5
  106.0 0.6 copy-start.6
